TPU v7x, 128 devices: a whole 4x4x4 slice. The times are simulated.
128 devices in a mesh: depth: 8 (over z, y_lo), height: 16 (over x, y_hi, core).
Axes of the slice: x: 4, y: 4 (y_hi: 2, y_lo: 2; y = y_hi * 2 + y_lo), z: 4, core: 2. Of those that a mesh axis runs over, the one named last changes fastest.
Arguments:
- volume: bfloat16 [32, 32, 128, 128], P(None, 'depth', 'height'), may hold values from -6 to 6
- filters_three: bfloat16 [27, 64, 32], replicated, may hold values from -0.21875 to 0.21875
- filters_four: bfloat16 [27, 128, 64], P(None, 'height'), may hold values from -0.15625 to 0.15625
- cotangent: bfloat16 [128, 16, 64, 64], P(None, 'depth', 'height'), may hold values from -6 to 6
Outputs:
- grad_volume: bfloat16 [32, 32, 128, 128], P(None, 'depth', 'height')
- grad_three: float32 [27, 64, 32], replicated
- grad_four: float32 [27, 128, 64], P(None, 'height')
All inputs are finite; a program needn't handle non-finite values.
Results may differ from a plain program's by a relative error of at most 0.023.
Values may be sent and summed in bfloat16 or wider, within the bound.
A program may use at most 256 MiB of HBM per device.

v0:
```python
import math

import jax
import jax.numpy as jnp
from jax import lax
from jax.sharding import PartitionSpec as P

TANH_SCALE = 0.7978845608028654
CUBIC_TERM = 0.044715


def extended_2(x, sides, width):
    for axis, dim in sides:
        size, length = (lax.axis_size(axis), x.shape[dim])
        up = [(i, (i + 1) % size) for i in range(size - 1)]
        down = [(j, i) for i, j in up]
        last = lax.slice_in_dim(x, length - width, length, axis=dim)
        first = lax.slice_in_dim(x, 0, width, axis=dim)
        before = lax.ppermute(last, axis, up)
        after = lax.ppermute(first, axis, down)
        x = jnp.concatenate([before, x, after], axis=dim)
    return x


def gelu_value(values_in):
    inner = jnp.tanh(TANH_SCALE * (values_in + CUBIC_TERM * values_in * values_in * values_in))
    return 0.5 * values_in * (1.0 + inner)


def gelu_slope(values_in):
    inner = jnp.tanh(TANH_SCALE * (values_in + CUBIC_TERM * values_in * values_in * values_in))
    return 0.5 * (1.0 + inner) + 0.5 * values_in * (1.0 - inner * inner) * TANH_SCALE * (
        1.0 + 3.0 * CUBIC_TERM * values_in * values_in
    )


def pad_width(values_in):
    return jnp.pad(values_in, ((0, 0), (0, 0), (0, 0), (1, 1)))


def forward_taps(padded, weights, depth_cells, height_cells, width_cells):
    running = jnp.zeros((weights.shape[1], depth_cells, height_cells, width_cells), jnp.float32)
    for first in range(3):
        for second in range(3):
            for third in range(3):
                window_piece = padded[
                    :,
                    first : first + depth_cells,
                    second : second + height_cells,
                    third : third + width_cells,
                ]
                running = running + jnp.einsum(
                    "oi,idhw->odhw",
                    weights[9 * first + 3 * second + third],
                    window_piece,
                    preferred_element_type=jnp.float32,
                )
    return running


def transpose_taps(padded, weights, depth_cells, height_cells, width_cells):
    running = jnp.zeros((weights.shape[2], depth_cells, height_cells, width_cells), jnp.float32)
    for first in range(3):
        for second in range(3):
            for third in range(3):
                window_piece = padded[
                    :,
                    2 - first : 2 - first + depth_cells,
                    2 - second : 2 - second + height_cells,
                    2 - third : 2 - third + width_cells,
                ]
                running = running + jnp.einsum(
                    "oi,odhw->idhw",
                    weights[9 * first + 3 * second + third],
                    window_piece,
                    preferred_element_type=jnp.float32,
                )
    return running


def weight_taps(delta, padded, depth_cells, height_cells, width_cells):
    collected = []
    for first in range(3):
        for second in range(3):
            for third in range(3):
                window_piece = padded[
                    :,
                    first : first + depth_cells,
                    second : second + height_cells,
                    third : third + width_cells,
                ]
                collected.append(
                    jnp.einsum(
                        "odhw,idhw->oi", delta, window_piece, preferred_element_type=jnp.float32
                    )
                )
    return jnp.stack(collected, axis=0)


def shards(volume, filters_three, filters_four, cotangent):
    channels_in, depth_cells, height_cells, width_cells = volume.shape
    depth_count = lax.axis_size("depth")
    height_count = lax.axis_size("height")
    scale_three = 1.0 / math.sqrt(
        depth_cells * depth_count * height_cells * height_count * width_cells
    )
    scale_four = 1.0 / math.sqrt(
        depth_cells * depth_count // 2 * (height_cells * height_count // 2) * (width_cells // 2)
    )
    half_depth = depth_cells // 2
    half_height = height_cells // 2
    half_width = width_cells // 2
    extended = extended_2(volume, (("depth", 1), ("height", 2)), 1)
    padded = pad_width(extended)
    act_three = forward_taps(padded, filters_three, depth_cells, height_cells, width_cells)
    channels_mid = act_three.shape[0]
    hidden = gelu_value(act_three).reshape(
        channels_mid, half_depth, 2, half_height, 2, half_width, 2
    )
    pooled = (jnp.sum(hidden, axis=(2, 4, 6)) * 0.125).astype(jnp.bfloat16)
    full_bank = lax.all_gather(filters_four, "height", axis=1, tiled=True)
    rimmed = extended_2(pooled, (("depth", 1), ("height", 2)), 1)
    pooled_pad = pad_width(rimmed)
    act_four = forward_taps(pooled_pad, full_bank, half_depth, half_height, half_width)
    delta_four = (cotangent.astype(jnp.float32) * gelu_slope(act_four)).astype(jnp.bfloat16)
    partial_four = weight_taps(delta_four, pooled_pad, half_depth, half_height, half_width)
    depth_summed = lax.psum(partial_four.astype(jnp.bfloat16), "depth")
    grad_four = (
        lax.psum_scatter(depth_summed, "height", scatter_dimension=1, tiled=True).astype(
            jnp.float32
        )
        * scale_four
    )
    delta_rim = extended_2(delta_four, (("depth", 1), ("height", 2)), 1)
    back_pooled = transpose_taps(
        pad_width(delta_rim), full_bank, half_depth, half_height, half_width
    )
    spread = (
        jnp.repeat(jnp.repeat(jnp.repeat(back_pooled, 2, axis=1), 2, axis=2), 2, axis=3) * 0.125
    )
    delta_three = (spread * gelu_slope(act_three)).astype(jnp.bfloat16)
    partial_three = weight_taps(delta_three, padded, depth_cells, height_cells, width_cells)
    grad_three = lax.psum(partial_three, ("depth", "height")) * scale_three
    delta_extended = extended_2(delta_three, (("depth", 1), ("height", 2)), 1)
    grad_volume = transpose_taps(
        pad_width(delta_extended), filters_three, depth_cells, height_cells, width_cells
    ).astype(jnp.bfloat16)
    return (grad_volume, grad_three, grad_four)


def solution(mesh):
    in_specs = (
        P(None, "depth", "height", None),
        P(),
        P(None, "height", None),
        P(None, "depth", "height", None),
    )
    out_specs = (P(None, "depth", "height", None), P(), P(None, "height", None))
    return jax.shard_map(shards, mesh=mesh, in_specs=in_specs, out_specs=out_specs, check_vma=False)
```

profile of v0, /device:TPU:1, one launch (start us, length us, event | category | flops | bytes accessed | tf_op | source)
XLA Modules:
  0.0 343.9 jit_solution(2866375884435285282)
XLA Ops:
  8.1 0.9 fusion.559
  9.0 4.0 %collective-permute-start = (bf16[32,1,8,128]{3,0,2,1:T(8,128)(2,1)S(1)}, bf16[32,1,8,128]{3,0,2,1:T(8,128)(2,1)S(1)}, u32[]{:S(2)}, u32[]{:S(2)}) collective-permute-start(bf16[32,1,8,128]{3,0,2,1:T(8,128)(2,1)S(1)} %copy.321), channel_id=1, source_target_pairs={{0,16},{16,32},{32,48},{48,64},{64,80},{80,96},{96,112},{1,17},{17... | collective-permute-start | bytes 196616 | tf_op jit(solution)/shard_map/ppermute | solution.py:19
  13.1 1.3 collective-permute-start.1
  14.4 1.2 constant_dynamic-update-slice_fusion.6
  15.6 2.6 collective-permute-done.1
  18.2 6.5 %collective-permute-start.2 = (bf16[32,6,1,128]{3,0,2,1:T(8,128)(2,1)S(1)}, bf16[32,6,1,128]{3,0,2,1:T(8,128)(2,1)S(1)}, u32[]{:S(2)}, u32[]{:S(2)}) collective-permute-start(bf16[32,6,1,128]{3,0,2,1:T(8,128)(2,1)S(1)} %get-tuple-element.18), channel_id=1, source_target_pairs={{0,1},{1,2},{2,3},{3,4},{4,5},{5,6},{6,7},{7,8},{8,9},{9,10},{10,1... | collective-permute-start | bytes 147464 | tf_op jit(solution)/shard_map/ppermute | solution.py:19
  24.8 1.9 collective-permute-start.3
  27.1 4.6 %collective-permute-done.3 = bf16[32,6,1,128]{3,0,2,1:T(8,128)(2,1)S(1)} collective-permute-done((bf16[32,6,1,128]{3,0,2,1:T(8,128)(2,1)S(1)}, bf16[32,6,1,128]{3,0,2,1:T(8,128)(2,1)S(1)}, u32[]{:S(2)}, u32[]{:S(2)}) %collective-permute-start.3) | collective-permute-done | bytes 49184 | tf_op jit(solution)/shard_map/ppermute | solution.py:20
  31.7 0.5 fusion.212
  32.5 0.4 fusion.320
  33.2 0.4 fusion.314
  34.0 0.4 fusion.308
  34.3 0.4 convolution_bitcast_fusion.10
  35.4 0.4 convolution_bitcast_fusion.8
  36.1 0.4 convolution_bitcast_fusion.4
  36.9 0.4 convolution_bitcast_fusion.6
  37.9 0.4 convolution_add_fusion.4
  39.7 0.4 fusion.24
  40.1 0.4 fusion.22
  40.5 0.7 fusion.27
  41.6 2.0 add_multiply_fusion
  43.6 1.8 copy.91
  45.4 2.4 reduce_sum.9
  47.8 1.0 multiply_convert_fusion
  48.8 3.9 %collective-permute-start.4 = (bf16[64,1,4,64]{0,3,2,1:T(8,128)(2,1)S(1)}, bf16[64,1,4,64]{0,3,2,1:T(8,128)(2,1)S(1)}, u32[]{:S(2)}, u32[]{:S(2)}) collective-permute-start(bf16[64,1,4,64]{0,3,2,1:T(8,128)(2,1)S(1)} %get-tuple-element.33), channel_id=1, source_target_pairs={{0,16},{16,32},{32,48},{48,64},{64,80},{80,96},{96,112},{1,17},{17... | collective-permute-start | bytes 98312 | tf_op jit(solution)/shard_map/ppermute | solution.py:19
  52.8 1.3 collective-permute-start.5
  54.1 25.2 %all_gather.3 = bf16[27,128,64]{2,1,0:T(8,128)(2,1)S(1)} all-gather(bf16[27,8,64]{2,1,0:T(8,128)(2,1)S(1)} %copy-done.14), channel_id=1, replica_groups=mesh['depth'=8,'height'=16] {'height'}, dimensions={1}, use_global_device_ids=true | all-gather | bytes 470016 | tf_op jit(solution)/shard_map/all_gather | solution.py:121
  79.3 1.9 collective-permute-start.6
  81.3 2.4 collective-permute-start.7
  83.9 4.5 %collective-permute-done.7 = bf16[64,4,1,64]{0,3,2,1:T(8,128)(2,1)S(1)} collective-permute-done((bf16[64,4,1,64]{0,3,2,1:T(8,128)(2,1)S(1)}, bf16[64,4,1,64]{0,3,2,1:T(8,128)(2,1)S(1)}, u32[]{:S(2)}, u32[]{:S(2)}) %collective-permute-start.7) | collective-permute-done | bytes 32800 | tf_op jit(solution)/shard_map/ppermute | solution.py:20
  93.8 0.4 fusion.283
  99.8 3.4 collective-permute-start.8
  103.2 1.3 collective-permute-start.9
  104.7 4.0 %collective-permute-done.9 = bf16[128,1,4,64]{0,3,2,1:T(8,128)(2,1)S(1)} collective-permute-done((bf16[128,1,4,64]{0,3,2,1:T(8,128)(2,1)S(1)}, bf16[128,1,4,64]{0,3,2,1:T(8,128)(2,1)S(1)}, u32[]{:S(2)}, u32[]{:S(2)}) %collective-permute-start.9) | collective-permute-done | bytes 65568 | tf_op jit(solution)/shard_map/ppermute | solution.py:20
  108.7 1.9 collective-permute-start.11
  110.7 5.1 %collective-permute-start.10 = (bf16[128,4,1,64]{0,3,2,1:T(8,128)(2,1)S(1)}, bf16[128,4,1,64]{0,3,2,1:T(8,128)(2,1)S(1)}, u32[]{:S(2)}, u32[]{:S(2)}) collective-permute-start(bf16[128,4,1,64]{0,3,2,1:T(8,128)(2,1)S(1)} %get-tuple-element.22), channel_id=1, source_target_pairs={{0,1},{1,2},{2,3},{3,4},{4,5},{5,6},{6,7},{7,8},{8,9},{9,10},{10,1... | collective-permute-start | bytes 196616 | tf_op jit(solution)/shard_map/ppermute | solution.py:19
  116.1 1.1 collective-permute-done.10
  122.3 0.4 broadcast_in_dim.10
  122.7 1.5 broadcast_in_dim.11
  124.1 2.2 copy.120
  126.3 1.9 fusion.210
  136.2 0.7 copy-done.12
  137.0 0.8 fusion.124
  137.8 3.3 copy.149
  141.4 1.3 collective-permute-start.13
  142.7 4.9 %collective-permute-start.12 = (bf16[64,1,8,128]{3,0,2,1:T(8,128)(2,1)S(1)}, bf16[64,1,8,128]{3,0,2,1:T(8,128)(2,1)S(1)}, u32[]{:S(2)}, u32[]{:S(2)}) collective-permute-start(bf16[64,1,8,128]{3,0,2,1:T(8,128)(2,1)S(1)} %get-tuple-element.16), channel_id=1, source_target_pairs={{0,16},{16,32},{32,48},{48,64},{64,80},{80,96},{96,112},{1,17},{17... | collective-permute-start | bytes 393224 | tf_op jit(solution)/shard_map/ppermute | solution.py:19
  147.6 137.9 %all-reduce.6.cloned.1.call-done = f32[27,64,32]{1,2,0:T(8,128)} async-done(((f32[27,64,32]{1,2,0:T(8,128)}), f32[27,64,32]{1,2,0:T(8,128)}) %all-reduce.6.cloned.1.call-update) | async-done | bytes 221200 | tf_op jit(solution)/shard_map/psum | solution.py:143
  285.5 1.8 broadcast_multiply_fusion
  287.3 5.1 %collective-permute-start.14 = (bf16[64,6,1,128]{3,0,2,1:T(8,128)(2,1)S(1)}, bf16[64,6,1,128]{3,0,2,1:T(8,128)(2,1)S(1)}, u32[]{:S(2)}, u32[]{:S(2)}) collective-permute-start(bf16[64,6,1,128]{3,0,2,1:T(8,128)(2,1)S(1)} %get-tuple-element.14), channel_id=1, source_target_pairs={{0,1},{1,2},{2,3},{3,4},{4,5},{5,6},{6,7},{7,8},{8,9},{9,10},{10,1... | collective-permute-start | bytes 294920 | tf_op jit(solution)/shard_map/ppermute | solution.py:19
  292.4 2.1 collective-permute-start.15
  295.0 4.9 %collective-permute-done.15 = bf16[64,6,1,128]{3,0,2,1:T(8,128)(2,1)S(1)} collective-permute-done((bf16[64,6,1,128]{3,0,2,1:T(8,128)(2,1)S(1)}, bf16[64,6,1,128]{3,0,2,1:T(8,128)(2,1)S(1)}, u32[]{:S(2)}, u32[]{:S(2)}) %collective-permute-start.15) | collective-permute-done | bytes 98336 | tf_op jit(solution)/shard_map/ppermute | solution.py:20
  300.5 1.8 select_maximum_fusion
  302.9 0.4 fusion.236
  303.4 0.4 fusion.242
  304.0 0.4 fusion.248
  305.0 0.4 fusion.227
  306.0 0.4 convolution_bitcast_fusion.15
  306.6 0.4 convolution_bitcast_fusion.18
  307.2 0.4 convolution_bitcast_fusion.21
  307.5 0.7 fusion.52
  308.5 0.4 fusion.53
  308.9 0.8 copy.150
  309.7 26.0 %psum.16 = bf16[27,8,64]{2,0,1:T(8,128)(2,1)S(1)} all-reduce(bf16[27,8,64]{2,0,1:T(8,128)(2,1)} %reduce-scatter.2.cloned.1.call-done), channel_id=1, replica_groups=mesh['depth'=8,'height'=16] {'depth'}, use_global_device_ids=true, to_apply=%region_2.3 | all-reduce | flops 13824 | bytes 55296 | tf_op jit(solution)/shard_map/psum | solution.py:127
  335.7 0.7 copy.151
  (203 shorter events, 33.9 us)
Async XLA Ops:
  8.0 18.7 %copy-start = (bf16[32,4,8,128]{3,2,1,0:T(8,128)(2,1)S(1)}, bf16[32,4,8,128]{3,2,1,0:T(8,128)(2,1)}, u32[]{:S(2)}) copy-start(bf16[32,4,8,128]{3,2,1,0:T(8,128)(2,1)} %param.4) | copy-start | bytes 786436
  8.0 18.7 %copy-start.6 = (bf16[27,64,32]{1,2,0:T(8,128)(2,1)S(1)}, bf16[27,64,32]{1,2,0:T(8,128)(2,1)}, u32[]{:S(2)}) copy-start(bf16[27,64,32]{1,2,0:T(8,128)(2,1)} %param.5) | copy-start | bytes 331780
  8.0 277.4 %all-reduce.6.cloned.1.call-start = ((), (), s32[]{:S(2)}) async-start(), calls=%async_computation.1 | async-start | bytes 884736 | tf_op jit(solution)/shard_map/psum | solution.py:143
  9.0 5.4 %collective-permute-start = (bf16[32,1,8,128]{3,0,2,1:T(8,128)(2,1)S(1)}, bf16[32,1,8,128]{3,0,2,1:T(8,128)(2,1)S(1)}, u32[]{:S(2)}, u32[]{:S(2)}) collective-permute-start(bf16[32,1,8,128]{3,0,2,1:T(8,128)(2,1)S(1)} %copy.321), channel_id=1, source_target_pairs={{0,16},{16,32},{32,48},{48,64},{64,80},{80,96},{96,112},{1,17},{17... | collective-permute-start | bytes 196616 | tf_op jit(solution)/shard_map/ppermute | solution.py:19
  13.1 5.1 %collective-permute-start.1 = (bf16[32,1,8,128]{3,0,2,1:T(8,128)(2,1)S(1)}, bf16[32,1,8,128]{3,0,2,1:T(8,128)(2,1)S(1)}, u32[]{:S(2)}, u32[]{:S(2)}) collective-permute-start(bf16[32,1,8,128]{3,0,2,1:T(8,128)(2,1)S(1)} %copy.322), channel_id=1, source_target_pairs={{16,0},{32,16},{48,32},{64,48},{80,64},{96,80},{112,96},{17,1},{33... | collective-permute-start | bytes 196616 | tf_op jit(solution)/shard_map/ppermute | solution.py:20
  15.6 23.1 %copy-start.4 = (bf16[32,5,8,128]{3,0,2,1:T(8,128)(2,1)}, bf16[32,5,8,128]{3,0,2,1:T(8,128)(2,1)S(1)}, u32[]{:S(2)}) copy-start(bf16[32,5,8,128]{3,0,2,1:T(8,128)(2,1)S(1)} %get-tuple-element.28) | copy-start | bytes 983044
  18.2 23.4 %copy-start.2 = (bf16[32,5,8,128]{3,0,2,1:T(8,128)(2,1)}, bf16[32,5,8,128]{3,0,2,1:T(8,128)(2,1)S(1)}, u32[]{:S(2)}) copy-start(bf16[32,5,8,128]{3,0,2,1:T(8,128)(2,1)S(1)} %get-tuple-element.35) | copy-start | bytes 983044
  18.2 8.8 %collective-permute-start.2 = (bf16[32,6,1,128]{3,0,2,1:T(8,128)(2,1)S(1)}, bf16[32,6,1,128]{3,0,2,1:T(8,128)(2,1)S(1)}, u32[]{:S(2)}, u32[]{:S(2)}) collective-permute-start(bf16[32,6,1,128]{3,0,2,1:T(8,128)(2,1)S(1)} %get-tuple-element.18), channel_id=1, source_target_pairs={{0,1},{1,2},{2,3},{3,4},{4,5},{5,6},{6,7},{7,8},{8,9},{9,10},{10,1... | collective-permute-start | bytes 147464 | tf_op jit(solution)/shard_map/ppermute | solution.py:19
  24.8 6.9 %collective-permute-start.3 = (bf16[32,6,1,128]{3,0,2,1:T(8,128)(2,1)S(1)}, bf16[32,6,1,128]{3,0,2,1:T(8,128)(2,1)S(1)}, u32[]{:S(2)}, u32[]{:S(2)}) collective-permute-start(bf16[32,6,1,128]{3,0,2,1:T(8,128)(2,1)S(1)} %get-tuple-element.19), channel_id=1, source_target_pairs={{1,0},{2,1},{3,2},{4,3},{5,4},{6,5},{7,6},{8,7},{9,8},{10,9},{11,1... | collective-permute-start | bytes 147464 | tf_op jit(solution)/shard_map/ppermute | solution.py:20
  27.0 13.1 %copy-start.10 = (bf16[32,6,1,128]{3,0,2,1:T(8,128)(2,1)}, bf16[32,6,1,128]{3,0,2,1:T(8,128)(2,1)S(1)}, u32[]{:S(2)}) copy-start(bf16[32,6,1,128]{3,0,2,1:T(8,128)(2,1)S(1)} %collective-permute-done.2) | copy-start | bytes 147460
  31.7 9.5 %copy-start.8 = (bf16[32,6,1,128]{3,0,2,1:T(8,128)(2,1)}, bf16[32,6,1,128]{3,0,2,1:T(8,128)(2,1)S(1)}, u32[]{:S(2)}) copy-start(bf16[32,6,1,128]{3,0,2,1:T(8,128)(2,1)S(1)} %collective-permute-done.3) | copy-start | bytes 147460
  45.4 8.7 %copy-start.14 = (bf16[27,8,64]{2,1,0:T(8,128)(2,1)S(1)}, bf16[27,8,64]{2,1,0:T(8,128)(2,1)}, u32[]{:S(2)}) copy-start(bf16[27,8,64]{2,1,0:T(8,128)(2,1)} %param.6) | copy-start | bytes 82948
  48.8 30.4 %collective-permute-start.4 = (bf16[64,1,4,64]{0,3,2,1:T(8,128)(2,1)S(1)}, bf16[64,1,4,64]{0,3,2,1:T(8,128)(2,1)S(1)}, u32[]{:S(2)}, u32[]{:S(2)}) collective-permute-start(bf16[64,1,4,64]{0,3,2,1:T(8,128)(2,1)S(1)} %get-tuple-element.33), channel_id=1, source_target_pairs={{0,16},{16,32},{32,48},{48,64},{64,80},{80,96},{96,112},{1,17},{17... | collective-permute-start | bytes 98312 | tf_op jit(solution)/shard_map/ppermute | solution.py:19
  52.8 26.5 %collective-permute-start.5 = (bf16[64,1,4,64]{0,3,2,1:T(8,128)(2,1)S(1)}, bf16[64,1,4,64]{0,3,2,1:T(8,128)(2,1)S(1)}, u32[]{:S(2)}, u32[]{:S(2)}) collective-permute-start(bf16[64,1,4,64]{0,3,2,1:T(8,128)(2,1)S(1)} %get-tuple-element.34), channel_id=1, source_target_pairs={{16,0},{32,16},{48,32},{64,48},{80,64},{96,80},{112,96},{17,1},{33... | collective-permute-start | bytes 98312 | tf_op jit(solution)/shard_map/ppermute | solution.py:20
  79.3 4.5 %collective-permute-start.6 = (bf16[64,4,1,64]{0,3,2,1:T(8,128)(2,1)S(1)}, bf16[64,4,1,64]{0,3,2,1:T(8,128)(2,1)S(1)}, u32[]{:S(2)}, u32[]{:S(2)}) collective-permute-start(bf16[64,4,1,64]{0,3,2,1:T(8,128)(2,1)S(1)} %get-tuple-element.24), channel_id=1, source_target_pairs={{0,1},{1,2},{2,3},{3,4},{4,5},{5,6},{6,7},{7,8},{8,9},{9,10},{10,1... | collective-permute-start | bytes 98312 | tf_op jit(solution)/shard_map/ppermute | solution.py:19
  81.3 7.1 %collective-permute-start.7 = (bf16[64,4,1,64]{0,3,2,1:T(8,128)(2,1)S(1)}, bf16[64,4,1,64]{0,3,2,1:T(8,128)(2,1)S(1)}, u32[]{:S(2)}, u32[]{:S(2)}) collective-permute-start(bf16[64,4,1,64]{0,3,2,1:T(8,128)(2,1)S(1)} %get-tuple-element.25), channel_id=1, source_target_pairs={{1,0},{2,1},{3,2},{4,3},{5,4},{6,5},{7,6},{8,7},{9,8},{10,9},{11,1... | collective-permute-start | bytes 98312 | tf_op jit(solution)/shard_map/ppermute | solution.py:20
  92.9 0.9 copy-start.15
  99.8 4.9 %collective-permute-start.8 = (bf16[128,1,4,64]{0,3,2,1:T(8,128)(2,1)S(1)}, bf16[128,1,4,64]{0,3,2,1:T(8,128)(2,1)S(1)}, u32[]{:S(2)}, u32[]{:S(2)}) collective-permute-start(bf16[128,1,4,64]{0,3,2,1:T(8,128)(2,1)S(1)} %get-tuple-element.31), channel_id=1, source_target_pairs={{0,16},{16,32},{32,48},{48,64},{64,80},{80,96},{96,112},{1,17},{17... | collective-permute-start | bytes 196616 | tf_op jit(solution)/shard_map/ppermute | solution.py:19
  103.2 5.5 %collective-permute-start.9 = (bf16[128,1,4,64]{0,3,2,1:T(8,128)(2,1)S(1)}, bf16[128,1,4,64]{0,3,2,1:T(8,128)(2,1)S(1)}, u32[]{:S(2)}, u32[]{:S(2)}) collective-permute-start(bf16[128,1,4,64]{0,3,2,1:T(8,128)(2,1)S(1)} %get-tuple-element.32), channel_id=1, source_target_pairs={{16,0},{32,16},{48,32},{64,48},{80,64},{96,80},{112,96},{17,1},{33... | collective-permute-start | bytes 196616 | tf_op jit(solution)/shard_map/ppermute | solution.py:20
  108.7 7.3 %collective-permute-start.11 = (bf16[128,4,1,64]{0,3,2,1:T(8,128)(2,1)S(1)}, bf16[128,4,1,64]{0,3,2,1:T(8,128)(2,1)S(1)}, u32[]{:S(2)}, u32[]{:S(2)}) collective-permute-start(bf16[128,4,1,64]{0,3,2,1:T(8,128)(2,1)S(1)} %get-tuple-element.23), channel_id=1, source_target_pairs={{1,0},{2,1},{3,2},{4,3},{5,4},{6,5},{7,6},{8,7},{9,8},{10,9},{11,1... | collective-permute-start | bytes 196616 | tf_op jit(solution)/shard_map/ppermute | solution.py:20
  110.7 6.5 %collective-permute-start.10 = (bf16[128,4,1,64]{0,3,2,1:T(8,128)(2,1)S(1)}, bf16[128,4,1,64]{0,3,2,1:T(8,128)(2,1)S(1)}, u32[]{:S(2)}, u32[]{:S(2)}) collective-permute-start(bf16[128,4,1,64]{0,3,2,1:T(8,128)(2,1)S(1)} %get-tuple-element.22), channel_id=1, source_target_pairs={{0,1},{1,2},{2,3},{3,4},{4,5},{5,6},{6,7},{7,8},{8,9},{9,10},{10,1... | collective-permute-start | bytes 196616 | tf_op jit(solution)/shard_map/ppermute | solution.py:19
  116.0 1.8 copy-start.13
  126.3 2.2 copy-start.11
  128.3 1.1 copy-start.5
  128.8 1.5 copy-start.9
  130.6 1.5 copy-start.1
  133.2 1.5 copy-start.3
  136.1 0.8 copy-start.12
  136.2 5.0 %copy-start.7 = (bf16[27,64,32]{1,2,0:T(8,128)(2,1)S(1)}, bf16[27,64,32]{1,2,0:T(8,128)(2,1)}, u32[]{:S(2)}) copy-start(bf16[27,64,32]{1,2,0:T(8,128)(2,1)} %param.5) | copy-start | bytes 331780
  136.9 172.8 %reduce-scatter.2.cloned.1.call-start = ((), (), s32[]{:S(2)}) async-start(), calls=%async_computation.2 | async-start | bytes 1114112 | tf_op jit(solution)/shard_map/reduce_scatter | solution.py:129
  141.4 145.9 %collective-permute-start.13 = (bf16[64,1,8,128]{3,0,2,1:T(8,128)(2,1)S(1)}, bf16[64,1,8,128]{3,0,2,1:T(8,128)(2,1)S(1)}, u32[]{:S(2)}, u32[]{:S(2)}) collective-permute-start(bf16[64,1,8,128]{3,0,2,1:T(8,128)(2,1)S(1)} %get-tuple-element.17), channel_id=1, source_target_pairs={{16,0},{32,16},{48,32},{64,48},{80,64},{96,80},{112,96},{17,1},{33... | collective-permute-start | bytes 393224 | tf_op jit(solution)/shard_map/ppermute | solution.py:20
  142.7 144.6 %collective-permute-start.12 = (bf16[64,1,8,128]{3,0,2,1:T(8,128)(2,1)S(1)}, bf16[64,1,8,128]{3,0,2,1:T(8,128)(2,1)S(1)}, u32[]{:S(2)}, u32[]{:S(2)}) collective-permute-start(bf16[64,1,8,128]{3,0,2,1:T(8,128)(2,1)S(1)} %get-tuple-element.16), channel_id=1, source_target_pairs={{0,16},{16,32},{32,48},{48,64},{64,80},{80,96},{96,112},{1,17},{17... | collective-permute-start | bytes 393224 | tf_op jit(solution)/shard_map/ppermute | solution.py:19
  287.3 7.7 %collective-permute-start.14 = (bf16[64,6,1,128]{3,0,2,1:T(8,128)(2,1)S(1)}, bf16[64,6,1,128]{3,0,2,1:T(8,128)(2,1)S(1)}, u32[]{:S(2)}, u32[]{:S(2)}) collective-permute-start(bf16[64,6,1,128]{3,0,2,1:T(8,128)(2,1)S(1)} %get-tuple-element.14), channel_id=1, source_target_pairs={{0,1},{1,2},{2,3},{3,4},{4,5},{5,6},{6,7},{7,8},{8,9},{9,10},{10,1... | collective-permute-start | bytes 294920 | tf_op jit(solution)/shard_map/ppermute | solution.py:19
  292.4 7.4 %collective-permute-start.15 = (bf16[64,6,1,128]{3,0,2,1:T(8,128)(2,1)S(1)}, bf16[64,6,1,128]{3,0,2,1:T(8,128)(2,1)S(1)}, u32[]{:S(2)}, u32[]{:S(2)}) collective-permute-start(bf16[64,6,1,128]{3,0,2,1:T(8,128)(2,1)S(1)} %get-tuple-element.15), channel_id=1, source_target_pairs={{1,0},{2,1},{3,2},{4,3},{5,4},{6,5},{7,6},{8,7},{9,8},{10,9},{11,1... | collective-permute-start | bytes 294920 | tf_op jit(solution)/shard_map/ppermute | solution.py:20
Sparse Core Ops, SparseCore 0:
  137.1 148.3 all-reduce.5
Sparse Core Ops, SparseCore 1:
  141.7 68.7 reduce-scatter.1
where the time goes:
time: 349 us; the launch traced here: 344 us
  waiting for transfers between devices  160 us (46%)
  blocking collectives  51.2 us (15%)
  starting transfers between devices  48.6 us (14%)
  matrix products  43.6 us (12%)
  between operations  16.6 us (5%)
  local copies, waits for them, and re-layouts  14.2 us (4%)
  other arithmetic  10.1 us (3%)
    psum x1, waiting for transfers between devices, shards(): grad_three = lax.psum(partial_three, ('depth', 'height')) * scale_three  138 us
    ppermute x8, starting transfers between devices, extended_2(): before = lax.ppermute(last, axis, up)  34.9 us
    psum x1, blocking collectives, shards(): depth_summed = lax.psum(partial_four.astype(jnp.bfloat16), 'depth')  26 us
    all_gather x1, blocking collectives, shards(): full_bank = lax.all_gather(filters_four, 'height', axis=1, tiled=True)  25.2 us
    ppermute x8, waiting for transfers between devices, extended_2(): after = lax.ppermute(first, axis, down)  20.5 us
    dot_general x54, matrix products, forward_taps(): jnp.einsum('oi,idhw->odhw', weights[9 * first + 3 * second + third], wind...  16.9 us
    dot_general x54, matrix products, weight_taps(): jnp.einsum('odhw,idhw->oi', delta, window_piece, preferred_element_type=j...  14.4 us
    ppermute x8, starting transfers between devices, extended_2(): after = lax.ppermute(first, axis, down)  13.6 us
  transfers between devices with their start and end apart: 18, of which 7 were waited for; matrix products, arithmetic and copies ran while one was open for 5% of the time, Pallas kernels for 0%

commit v1 on v0

v1 whole, which is shorter than its diff:
```python
import functools
import math

import jax
import jax.numpy as jnp
from jax import lax
from jax.experimental import pallas as pl
from jax.experimental.pallas import tpu as pltpu
from jax.sharding import PartitionSpec as P

TANH_SCALE = 0.7978845608028654
CUBIC_TERM = 0.044715
MESH = pl.DeviceIdType.MESH
F32 = jnp.float32
BF16 = jnp.bfloat16

ND = 8
NH = 16
DIRECTIONS = [(dd, hh) for dd in (-1, 0, 1) for hh in (-1, 0, 1) if (dd, hh) != (0, 0)]


def gelu_parts(v):
    u = v * v
    inner = jnp.tanh(TANH_SCALE * (v + CUBIC_TERM * v * u))
    half = 0.5 * (1.0 + inner)
    value = v * half
    slope = half + 0.5 * v * (1.0 - inner * inner) * TANH_SCALE * (1.0 + 3.0 * CUBIC_TERM * u)
    return value, slope


def lanes_iota(shape):
    return lax.broadcasted_iota(jnp.int32, shape, len(shape) - 1)


def shifted(v, step):
    lane = lanes_iota(v.shape)
    before = jnp.where(lane < step, 0.0, pltpu.roll(v, step, 1))
    after = jnp.where(lane >= 128 - step, 0.0, pltpu.roll(v, 128 - step, 1))
    return before, after


def stack_width(row, step):
    before, after = shifted(row.astype(F32), step)
    return jnp.concatenate([before.astype(BF16), row, after.astype(BF16)], axis=0)


def part(at, cells, far):
    if at == 0:
        return pl.ds(1, cells)
    if at < 0:
        return pl.ds(cells + 1, 1) if far else pl.ds(1, 1)
    return pl.ds(0, 1) if far else pl.ds(cells, 1)


def kernel(
    x_in, a3, a6, f4, cot,
    gv_out, g3_out, g4_out,
    xb, xx, slope3, pb, pp, d4, d3, bank, a4, a5,
    f4acc, r4, q4, t4, q4b,
    f3acc, r3, q3, t3, q3b, v3,
    halo_s, halo_r, ag_s, ag_r, s4_s, s4_r, b4_s, b4_r, s3_s, s3_r, b3_s, b3_r, c3_s, c3_r,
):
    d = lax.axis_index("depth")
    h = lax.axis_index("height")

    def dev_d(k):
        return (lax.rem(d + k + ND, ND), h)

    def dev_h(k):
        return (d, lax.rem(h + k + NH, NH))

    barrier = pltpu.get_barrier_semaphore()
    for k in range(1, NH):
        pl.semaphore_signal(barrier, inc=1, device_id=dev_h(k), device_id_type=MESH)
    for k in range(1, ND):
        pl.semaphore_signal(barrier, inc=1, device_id=dev_d(k), device_id_type=MESH)
    for dd in (-1, 1):
        for hh in (-1, 1):
            pl.semaphore_signal(
                barrier,
                inc=1,
                device_id=(lax.rem(d + dd + ND, ND), lax.rem(h + hh + NH, NH)),
                device_id_type=MESH,
            )
    pl.semaphore_wait(barrier, NH - 1 + ND - 1 + 4)

    def halo_copy(which, n, buf, cells_d, cells_h):
        dd, hh = DIRECTIONS[n]
        return pltpu.make_async_remote_copy(
            src_ref=buf.at[part(dd, cells_d, False), part(hh, cells_h, False)],
            dst_ref=buf.at[part(dd, cells_d, True), part(hh, cells_h, True)],
            send_sem=halo_s.at[which, n],
            recv_sem=halo_r.at[which, n],
            device_id=(lax.rem(d + dd + ND, ND), lax.rem(h + hh + NH, NH)),
            device_id_type=MESH,
        )

    def halo_start(which, buf, cells_d, cells_h):
        for n in range(8):
            halo_copy(which, n, buf, cells_d, cells_h).start()

    def halo_wait(which, buf, cells_d, cells_h):
        for n in range(8):
            halo_copy(which, n, buf, cells_d, cells_h).wait_send()
        for n in range(8):
            halo_copy(which, n, buf, cells_d, cells_h).wait_recv()
        channels = buf.shape[2]

        @pl.when(d == 0)
        def _():
            buf[0] = jnp.zeros((cells_h + 2, channels, 128), BF16)

        @pl.when(d == ND - 1)
        def _():
            buf[cells_d + 1] = jnp.zeros((cells_h + 2, channels, 128), BF16)

        @pl.when(h == 0)
        def _():
            buf[:, 0] = jnp.zeros((cells_d + 2, channels, 128), BF16)

        @pl.when(h == NH - 1)
        def _():
            buf[:, cells_h + 1] = jnp.zeros((cells_d + 2, channels, 128), BF16)

    def scatter_h(src, dst, send, recv, k):
        other = lax.rem(h + k, NH)
        return pltpu.make_async_remote_copy(
            src_ref=src.at[other],
            dst_ref=dst.at[k],
            send_sem=send.at[k],
            recv_sem=recv.at[k],
            device_id=(d, other),
            device_id_type=MESH,
        )

    def share_d(src, dst, send, recv, k):
        return pltpu.make_async_remote_copy(
            src_ref=src,
            dst_ref=dst.at[k],
            send_sem=send.at[k],
            recv_sem=recv.at[k],
            device_id=(lax.rem(d + k, ND), h),
            device_id_type=MESH,
        )

    def gather_send(src, dst, send, recv, k):
        return pltpu.make_async_remote_copy(
            src_ref=src,
            dst_ref=dst.at[h],
            send_sem=send.at[k],
            recv_sem=recv.at[k],
            device_id=(d, lax.rem(h + k, NH)),
            device_id_type=MESH,
        )

    def gather_recv(src, dst, send, recv, k):
        return pltpu.make_async_remote_copy(
            src_ref=src,
            dst_ref=dst.at[lax.rem(h - k + NH, NH)],
            send_sem=send.at[k],
            recv_sem=recv.at[k],
            device_id=(d, lax.rem(h + k, NH)),
            device_id_type=MESH,
        )

    def each(low, high, body):
        def step(k, carry):
            body(k)
            return carry

        lax.fori_loop(low, high, step, 0)

    xb[1:5, 1:9] = x_in[...]
    halo_start(0, xb, 4, 8)
    each(1, NH, lambda k: gather_send(f4, bank, ag_s, ag_r, k).start())
    bank[h] = f4[...]

    def stack_x(i):
        for j in range(10):
            xx[i, j] = stack_width(xb[i, j], 1)

    halo_wait(0, xb, 4, 8)
    each(0, 6, stack_x)

    def forward3(i):
        for j in range(4):
            total = None
            for di in range(2):
                cols = [
                    jnp.concatenate(
                        [xx[2 * i + di + a, 2 * j + s + b] for a in range(3) for b in range(3)],
                        axis=0,
                    )
                    for s in range(2)
                ]
                act = jnp.dot(
                    a3[...], jnp.concatenate(cols, axis=1), preferred_element_type=F32
                )
                value, slope = gelu_parts(act)
                for s in range(2):
                    slope3[2 * i + di, 2 * j + s] = slope[:, 128 * s : 128 * s + 128]
                both = value[:, :128] + value[:, 128:]
                total = both if total is None else total + both
            total = (total + pltpu.roll(total, 127, 1)) * 0.125
            even = lanes_iota(total.shape) % 2 == 0
            pb[1 + i, 1 + j] = jnp.where(even, total, 0.0).astype(BF16)

    each(0, 2, forward3)
    halo_start(1, pb, 2, 4)

    def wait_gather(k):
        gather_send(f4, bank, ag_s, ag_r, k).wait_send()
        gather_recv(f4, bank, ag_s, ag_r, k).wait_recv()

    each(1, NH, wait_gather)
    wide = [bank[s].astype(F32) for s in range(NH)]
    low = jnp.concatenate([w[:8] for w in wide], axis=0)
    high = jnp.concatenate([w[8:] for w in wide], axis=0)
    a4[...] = jnp.concatenate([low, high], axis=1).astype(BF16)
    for ab in range(9):
        a5[:, 128 * ab : 128 * ab + 128] = jnp.transpose(
            a4[:, 192 * ab : 192 * ab + 192].astype(F32)
        ).astype(BF16)

    halo_wait(1, pb, 2, 4)

    def stack_p(i):
        for j in range(6):
            pp[i, j] = stack_width(pb[i, j], 2)

    each(0, 4, stack_p)

    def forward4(i):
        for j in range(2):
            cols = [
                jnp.concatenate(
                    [pp[i + a, 2 * j + s + b] for a in range(3) for b in range(3)], axis=0
                )
                for s in range(2)
            ]
            act = jnp.dot(
                a4[:, :1728], jnp.concatenate(cols, axis=1), preferred_element_type=F32
            )
            _, slope = gelu_parts(act)
            for s in range(2):
                d4[1 + i, 1 + 2 * j + s] = (
                    cot[i, 2 * j + s].astype(F32) * slope[:, 128 * s : 128 * s + 128]
                ).astype(BF16)

    each(0, 2, forward4)
    halo_start(2, d4, 2, 4)

    cells4 = [(i, j) for i in range(2) for j in range(4)]
    left4 = jnp.concatenate([d4[1 + i, 1 + j] for i, j in cells4], axis=1)
    for g in range(5):
        taps = [ab for ab in (2 * g, 2 * g + 1) if ab < 9]
        right = jnp.concatenate(
            [
                jnp.concatenate([pp[i + ab // 3, j + ab % 3] for i, j in cells4], axis=1)
                for ab in taps
            ],
            axis=0,
        )
        piece = lax.dot_general(
            left4, right, (((1,), (1,)), ((), ())), preferred_element_type=F32
        )
        if len(taps) == 1:
            piece = jnp.concatenate([piece, jnp.zeros((128, 64), F32)], axis=1)
        f4acc[:, 384 * g : 384 * g + piece.shape[1]] = piece

    def pack4(s):
        rows = pl.ds(pl.multiple_of(8 * s, 8), 8)
        r4[s] = jnp.concatenate([f4acc[rows, :896], f4acc[rows, 896:]], axis=0).astype(BF16)

    each(0, NH, pack4)
    each(1, NH, lambda k: scatter_h(r4, q4, s4_s, s4_r, k).start())

    halo_wait(2, d4, 2, 4)

    def back4(i):
        for j in range(2):
            cols = [
                jnp.concatenate(
                    [d4[i + 2 - a, 2 * j + s + 2 - b] for a in range(3) for b in range(3)], axis=0
                )
                for s in range(2)
            ]
            y = jnp.dot(a5[...], jnp.concatenate(cols, axis=1), preferred_element_type=F32)
            for s in range(2):
                ys = y[:, 128 * s : 128 * s + 128]
                _, from_after = shifted(ys[:64], 2)
                from_before, _ = shifted(ys[128:], 2)
                back = (ys[64:128] + from_after + from_before) * 0.125
                spread = back + pltpu.roll(back, 1, 1)
                for di in range(2):
                    for dj in range(2):
                        row, col = 2 * i + di, 2 * (2 * j + s) + dj
                        d3[1 + row, 1 + col] = (spread * slope3[row, col]).astype(BF16)

    each(0, 2, back4)
    halo_start(3, d3, 4, 8)

    f3acc[...] = jnp.zeros(f3acc.shape, F32)

    def weight3(i):
        left = jnp.concatenate([d3[1 + i, 1 + j] for j in range(8)], axis=1)
        right = jnp.concatenate(
            [
                jnp.concatenate([xx[i + a, j + b] for j in range(8)], axis=1)
                for a in range(3)
                for b in range(3)
            ],
            axis=0,
        )
        f3acc[:, :864] += lax.dot_general(
            left, right, (((1,), (1,)), ((), ())), preferred_element_type=F32
        )

    each(0, 4, weight3)
    for c in range(16):
        r3[c] = f3acc[
            16 * (c % 4) : 16 * (c % 4) + 16, 256 * (c // 4) : 256 * (c // 4) + 256
        ].astype(BF16)
    each(1, NH, lambda k: scatter_h(r3, q3, s3_s, s3_r, k).start())

    def wait_4(k):
        copy = scatter_h(r4, q4, s4_s, s4_r, k)
        copy.wait_send()
        copy.wait_recv()

    each(1, NH, wait_4)
    total4 = r4[h].astype(F32)
    for k in range(1, NH):
        total4 = total4 + q4[k].astype(F32)
    t4[...] = total4.astype(BF16)
    each(1, ND, lambda k: share_d(t4, q4b, b4_s, b4_r, k).start())

    halo_wait(3, d3, 4, 8)

    def back3(i):
        for j in range(4):
            cols = [
                jnp.concatenate(
                    [d3[i + 2 - a, 2 * j + s + 2 - b] for a in range(3) for b in range(3)], axis=0
                )
                for s in range(2)
            ]
            y = jnp.dot(a6[...], jnp.concatenate(cols, axis=1), preferred_element_type=F32)
            for s in range(2):
                ys = y[:, 128 * s : 128 * s + 128]
                _, from_after = shifted(ys[:32], 1)
                from_before, _ = shifted(ys[64:], 1)
                gv_out[i, 2 * j + s] = (ys[32:64] + from_after + from_before).astype(BF16)

    def wait_3(k):
        copy = scatter_h(r3, q3, s3_s, s3_r, k)
        copy.wait_send()
        copy.wait_recv()

    each(1, NH, wait_3)
    total3 = r3[h].astype(F32)
    for k in range(1, NH):
        total3 = total3 + q3[k].astype(F32)
    t3[...] = total3
    each(1, ND, lambda k: share_d(t3, q3b, b3_s, b3_r, k).start())

    each(0, 4, back3)

    def wait_b3(k):
        copy = share_d(t3, q3b, b3_s, b3_r, k)
        copy.wait_send()
        copy.wait_recv()

    each(1, ND, wait_b3)
    whole3 = t3[...]
    for k in range(1, ND):
        whole3 = whole3 + q3b[k]
    v3[h] = (whole3 * (1.0 / math.sqrt(32 * 128 * 128))).astype(BF16)
    each(1, NH, lambda k: gather_send(v3.at[h], v3, c3_s, c3_r, k).start())

    def wait_b4(k):
        copy = share_d(t4, q4b, b4_s, b4_r, k)
        copy.wait_send()
        copy.wait_recv()

    each(1, ND, wait_b4)
    whole4 = t4[...].astype(F32)
    for k in range(1, ND):
        whole4 = whole4 + q4b[k].astype(F32)
    g4_out[...] = whole4 * (1.0 / math.sqrt(16 * 64 * 64))

    def wait_c3(k):
        gather_send(v3.at[h], v3, c3_s, c3_r, k).wait_send()
        gather_recv(v3.at[h], v3, c3_s, c3_r, k).wait_recv()

    each(1, NH, wait_c3)
    for c in range(16):
        g3_out[16 * (c % 4) : 16 * (c % 4) + 16, 256 * (c // 4) : 256 * (c // 4) + 256] = v3[
            c
        ].astype(F32)


def shards(volume, filters_three, filters_four, cotangent):
    x_in = jnp.transpose(volume, (1, 2, 0, 3))
    a3 = jnp.transpose(filters_three, (1, 0, 2)).reshape(64, 864)
    a6 = jnp.transpose(filters_three.reshape(9, 3, 64, 32), (1, 3, 0, 2)).reshape(96, 576)
    f4 = jnp.pad(jnp.transpose(filters_four, (1, 0, 2)).reshape(8, 1728), ((0, 0), (0, 64)))
    f4 = jnp.transpose(f4.reshape(8, 2, 896), (1, 0, 2)).reshape(16, 896)
    cot = jnp.transpose(cotangent, (1, 2, 0, 3))
    cot = lax.pad(cot, jnp.zeros((), BF16), ((0, 0, 0), (0, 0, 0), (0, 0, 0), (0, 1, 1)))

    vmem = pl.BlockSpec(memory_space=pltpu.VMEM)
    dma = pltpu.SemaphoreType.DMA
    gv, g3, g4 = pl.pallas_call(
        kernel,
        out_shape=(
            jax.ShapeDtypeStruct((4, 8, 32, 128), BF16),
            jax.ShapeDtypeStruct((64, 1024), F32),
            jax.ShapeDtypeStruct((16, 896), F32),
        ),
        in_specs=[vmem] * 5,
        out_specs=(vmem,) * 3,
        scratch_shapes=[
            pltpu.VMEM((6, 10, 32, 128), BF16),
            pltpu.VMEM((6, 10, 96, 128), BF16),
            pltpu.VMEM((4, 8, 64, 128), F32),
            pltpu.VMEM((4, 6, 64, 128), BF16),
            pltpu.VMEM((4, 6, 192, 128), BF16),
            pltpu.VMEM((4, 6, 128, 128), BF16),
            pltpu.VMEM((6, 10, 64, 128), BF16),
            pltpu.VMEM((16, 16, 896), BF16),
            pltpu.VMEM((128, 1792), BF16),
            pltpu.VMEM((192, 1152), BF16),
            pltpu.VMEM((128, 1792), F32),
            pltpu.VMEM((16, 16, 896), BF16),
            pltpu.VMEM((16, 16, 896), BF16),
            pltpu.VMEM((16, 896), BF16),
            pltpu.VMEM((8, 16, 896), BF16),
            pltpu.VMEM((64, 1024), F32),
            pltpu.VMEM((16, 16, 256), BF16),
            pltpu.VMEM((16, 16, 256), BF16),
            pltpu.VMEM((16, 256), F32),
            pltpu.VMEM((8, 16, 256), F32),
            pltpu.VMEM((16, 16, 256), BF16),
            dma((4, 8)),
            dma((4, 8)),
            dma((16,)),
            dma((16,)),
            dma((16,)),
            dma((16,)),
            dma((8,)),
            dma((8,)),
            dma((16,)),
            dma((16,)),
            dma((8,)),
            dma((8,)),
            dma((16,)),
            dma((16,)),
        ],
        compiler_params=pltpu.CompilerParams(
            collective_id=0, has_side_effects=True, vmem_limit_bytes=40 * 1024 * 1024
        ),
    )(x_in, a3, a6, f4, cot)

    grad_volume = jnp.transpose(gv, (2, 0, 1, 3))
    grad_three = jnp.transpose(g3[:, :864].reshape(64, 27, 32), (1, 0, 2))
    g4 = jnp.transpose(g4.reshape(2, 8, 896), (1, 0, 2)).reshape(8, 1792)
    grad_four = jnp.transpose(g4[:, :1728].reshape(8, 27, 64), (1, 0, 2))
    return (grad_volume, grad_three, grad_four)


def solution(mesh):
    in_specs = (
        P(None, "depth", "height", None),
        P(),
        P(None, "height", None),
        P(None, "depth", "height", None),
    )
    out_specs = (P(None, "depth", "height", None), P(), P(None, "height", None))
    return jax.shard_map(shards, mesh=mesh, in_specs=in_specs, out_specs=out_specs, check_vma=False)
```

time: 349 us -> 80.5 us (0.23); the launches traced: 344 us -> 80.3 us
  waiting for transfers between devices: 160 us -> 0 us
  Pallas kernels: 0 us -> 68.9 us
  blocking collectives: 51.2 us -> 0 us
  starting transfers between devices: 48.6 us -> 0 us
  matrix products: 43.6 us -> 0 us
  between operations: 16.6 us -> 0.7 us
  other arithmetic: 10.1 us -> 0 us
    psum x1 -> x0, waiting for transfers between devices: 138 us -> none  [shards(): grad_three = lax.psum(partial_three, ('depth', 'height')) * scale_three]
    pallas_call x0 -> x1, Pallas kernels: none -> 68.9 us  [shards(): pl.pallas_call(kernel, out_shape=(jax.ShapeDtypeStruct((4, 8, 32, 128), B...]
    ppermute x16 -> x0, starting transfers between devices: 48.5 us -> none  [the longest x8 34.9 us: extended_2(): before = lax.ppermute(last, axis, up)]
    dot_general x162 -> x0, matrix products: 43.6 us -> none  [the longest x54 16.9 us: forward_taps(): jnp.einsum('oi,idhw->odhw', weights[9 * first + 3 * second + third], wind...]
    psum x1 -> x0, blocking collectives: 26 us -> none  [shards(): depth_summed = lax.psum(partial_four.astype(jnp.bfloat16), 'depth')]
    all_gather x1 -> x0, blocking collectives: 25.2 us -> none  [shards(): full_bank = lax.all_gather(filters_four, 'height', axis=1, tiled=True)]
    ppermute x16 -> x0, waiting for transfers between devices: 21.6 us -> none  [the longest x8 20.5 us: extended_2(): after = lax.ppermute(first, axis, down)]
    pad x0 -> x2, local copies, waits for them, and re-layouts: none -> 4.92 us  [the longest x1 4.92 us: shards(): lax.pad(cot, jnp.zeros((), BF16), ((0, 0, 0), (0, 0, 0), (0, 0, 0), (0, 1...]
  transfers between devices with their start and end apart: 18 -> 0, of which waited for: 7 -> 0; matrix products, arithmetic and copies ran while one was open for 5% -> 0% of each run, Pallas kernels for 0% -> 0%
where the time goes in v1:
time: 80.5 us; the launch traced here: 80.3 us
  Pallas kernels  68.9 us (86%)
  local copies, waits for them, and re-layouts  10.8 us (13%)
    pallas_call x1, Pallas kernels, shards(): pl.pallas_call(kernel, out_shape=(jax.ShapeDtypeStruct((4, 8, 32, 128), B...  68.9 us
    pad x1, local copies, waits for them, and re-layouts, shards(): lax.pad(cot, jnp.zeros((), BF16), ((0, 0, 0), (0, 0, 0), (0, 0, 0), (0, 1...  4.92 us
    unnamed x10, local copies, waits for them, and re-layouts  3.28 us

profile of v1, /device:TPU:1, one launch (start us, length us, event | category | flops | bytes accessed | tf_op | source)
XLA Modules:
  0.0 80.3 jit_solution(2029837899451220624)
XLA Ops:
  0.6 0.0 copy-start
  0.6 0.9 %copy.15 = bf16[8,27,64]{2,1,0:T(8,128)(2,1)S(1)} copy(bf16[8,27,64]{2,0,1:T(8,128)(2,1)} %bitcast.38) | data formatting | bytes 55296 | tf_op jit(solution)/shard_map/transpose | solution.py:407
  1.5 0.0 copy-start.1
  1.5 0.1 reshape.39
  1.7 0.0 copy-done
  1.7 0.1 copy.17.a3
  1.8 0.7 copy-done.1
  2.5 0.0 copy-start.2
  2.5 0.1 copy.24
  2.6 0.8 copy-done.2
  3.4 0.2 copy.16
  3.6 4.9 %pad.8.cot = bf16[2,4,128,128]{3,2,1,0:T(8,128)(2,1)S(1)} pad(bf16[2,4,128,64]{3,2,1,0:T(8,128)(2,1)S(1)} %bitcast.33, bf16[]{:T(256)} %constant.1.clone.1), padding=0_0_0x0_0_0x0_0_0x0_1_1 | pad | bytes 393218 | tf_op jit(solution)/shard_map/pad | solution.py:410
  8.5 0.1 copy.23
  8.6 0.2 reshape.38.a6
  8.9 68.9 %shard_map.67 = (bf16[4,8,32,128]{3,2,1,0:T(8,128)(2,1)S(1)}, f32[64,1024]{1,0:T(8,128)S(1)}, f32[16,896]{1,0:T(8,128)S(1)}) custom-call(bf16[4,8,32,128]{3,2,1,0:T(8,128)(2,1)S(1)} %bitcast.28, bf16[64,864]{1,0:T(8,128)(2,1)S(1)} %copy.17.a3, bf16[96,576]{1,0:T(8,128)(2,1)S(1)} %reshape.38.a6, bf16[16,896]{1,0:T(8,128)(2,1)S(1)} %bitcast.30, ...), custom_call_target="tpu_custom_call" | custom-call | tf_op jit(solution)/shard_map/pallas_call | solution.py:414
  77.7 0.8 %copy.19 = bf16[32,4,8,128]{3,2,1,0:T(8,128)(2,1)} copy(bf16[32,4,8,128]{3,0,2,1:T(8,128)(2,1)S(1)} %bitcast.29) | data formatting | bytes 524288
  78.5 0.1 reshape.45
  78.6 0.7 copy.20
  79.4 1.0 %copy.18 = f32[64,864]{0,1:T(8,128)} copy(f32[64,864]{1,0:T(8,128)S(1)} %slice.6) | data formatting | bytes 442368 | tf_op jit(solution)/shard_map/slice | solution.py:466
  (2 shorter events, 0.0 us)
Async XLA Ops:
  0.6 1.0 %copy-start = (bf16[27,64,32]{1,2,0:T(8,128)(2,1)S(1)}, bf16[27,64,32]{1,2,0:T(8,128)(2,1)}, u32[]{:S(2)}) copy-start(bf16[27,64,32]{1,2,0:T(8,128)(2,1)} %param.5) | copy-start | bytes 331780
  1.5 1.0 %copy-start.1 = (bf16[32,4,8,128]{3,2,1,0:T(8,128)(2,1)S(1)}, bf16[32,4,8,128]{3,2,1,0:T(8,128)(2,1)}, u32[]{:S(2)}) copy-start(bf16[32,4,8,128]{3,2,1,0:T(8,128)(2,1)} %param.4) | copy-start | bytes 786436
  2.5 0.9 %copy-start.2 = (bf16[128,2,4,64]{0,3,2,1:T(8,128)(2,1)S(1)}, bf16[128,2,4,64]{0,3,2,1:T(8,128)(2,1)}, u32[]{:S(2)}) copy-start(bf16[128,2,4,64]{0,3,2,1:T(8,128)(2,1)} %param.7) | copy-start | bytes 393220

commit v2 on v1

v2 whole, which is shorter than its diff:
```python
import functools
import math

import jax
import jax.numpy as jnp
from jax import lax
from jax.experimental import pallas as pl
from jax.experimental.pallas import tpu as pltpu
from jax.sharding import PartitionSpec as P

TANH_SCALE = 0.7978845608028654
CUBIC_TERM = 0.044715
MESH = pl.DeviceIdType.MESH
F32 = jnp.float32
BF16 = jnp.bfloat16

ND = 8
NH = 16
DIRECTIONS = [(dd, hh) for dd in (-1, 0, 1) for hh in (-1, 0, 1) if (dd, hh) != (0, 0)]


def gelu_parts(v):
    u = v * v
    inner = jnp.tanh(TANH_SCALE * (v + CUBIC_TERM * v * u))
    half = 0.5 * (1.0 + inner)
    value = v * half
    slope = half + 0.5 * v * (1.0 - inner * inner) * TANH_SCALE * (1.0 + 3.0 * CUBIC_TERM * u)
    return value, slope


def stage(name, body):
    body()


def lanes_iota(shape):
    return lax.broadcasted_iota(jnp.int32, shape, len(shape) - 1)


def shifted(v, step):
    lane = lanes_iota(v.shape)
    before = jnp.where(lane < step, 0.0, pltpu.roll(v, step, 1))
    after = jnp.where(lane >= 128 - step, 0.0, pltpu.roll(v, 128 - step, 1))
    return before, after


def stack_width(row, step):
    before, after = shifted(row.astype(F32), step)
    return jnp.concatenate([before.astype(BF16), row, after.astype(BF16)], axis=0)


def part(at, cells, width, far):
    if at == 0:
        return pl.ds(width, cells)
    if at < 0:
        return pl.ds(cells + width, width) if far else pl.ds(width, width)
    return pl.ds(0, width) if far else pl.ds(cells, width)


def interleave(even_row, odd_row):
    even = lanes_iota(even_row.shape) % 2 == 0
    return jnp.where(even, even_row, pltpu.roll(odd_row, 1, 1))


def interleave_odd(even_row, odd_row):
    even = lanes_iota(even_row.shape) % 2 == 0
    return jnp.where(even, pltpu.roll(even_row, 127, 1), odd_row)


def two_rows(first, second):
    return jnp.concatenate([interleave(first, second), interleave_odd(first, second)], axis=0)


def kernel(
    x_in, a3, a6, f4, cot,
    gv_out, g3_out, g4_out,
    xb, xx, slope3, ck, pk, pq, dq, dv, d3, bank, a4, a5,
    f4acc, r4, q4, t4, q4b,
    f3acc, r3, q3, t3, q3b, v3,
    halo_s, halo_r, ag_s, ag_r, s4_s, s4_r, b4_s, b4_r, s3_s, s3_r, b3_s, b3_r, c3_s, c3_r,
):
    d = lax.axis_index("depth")
    h = lax.axis_index("height")

    def around(dd, hh):
        return (lax.rem(d + dd + ND, ND), lax.rem(h + hh + NH, NH))

    def partner(other):
        flip = lax.rem(lax.rem(h, 4) // 2 + lax.rem(other, 4) // 2, 2)
        return (d + flip * (1 - 2 * lax.rem(d, 2)), other)

    def each(low, high, body):
        def step(k, carry):
            body(k)
            return carry

        lax.fori_loop(low, high, step, 0)

    barrier = pltpu.get_barrier_semaphore()

    def greet(device):
        pl.semaphore_signal(barrier, inc=1, device_id=device, device_id_type=MESH)

    for dd, hh in DIRECTIONS:
        greet(around(dd, hh))
    for k in range(1, NH):
        greet(partner(lax.rem(h + k, NH)))
    for k in range(2, ND - 1):
        greet(around(k, 0))

    def dilate():
        at = 2 * lax.broadcasted_iota(jnp.int32, (64, 128), 0)
        lane = lanes_iota((64, 128))
        to_even = (lane == at).astype(F32).astype(BF16)
        to_odd = (lane == at + 1).astype(F32).astype(BF16)
        for i in range(2):
            for j in range(4):
                row = cot[i, j]
                ck[1 + i, 1 + j] = (
                    jnp.dot(row[:64], to_even, preferred_element_type=F32)
                    + jnp.dot(row[64:], to_odd, preferred_element_type=F32)
                ).astype(BF16)

    xb[1:5, 1:9] = x_in[...]
    stage("dilate", dilate)
    pl.semaphore_wait(barrier, 8 + NH - 1 + ND - 3)

    def halo_copy(which, n, buf, cells_d, cells_h, width):
        dd, hh = DIRECTIONS[n]
        return pltpu.make_async_remote_copy(
            src_ref=buf.at[part(dd, cells_d, width, False), part(hh, cells_h, width, False)],
            dst_ref=buf.at[part(dd, cells_d, width, True), part(hh, cells_h, width, True)],
            send_sem=halo_s.at[which, n],
            recv_sem=halo_r.at[which, n],
            device_id=around(dd, hh),
            device_id_type=MESH,
        )

    def halo_start(*which):
        for n in range(8):
            halo_copy(which[0], n, *which[1:]).start()

    def halo_wait(*which):
        for n in range(8):
            halo_copy(which[0], n, *which[1:]).wait_send()
        for n in range(8):
            halo_copy(which[0], n, *which[1:]).wait_recv()
        _, buf, cells_d, cells_h, width = which
        channels = buf.shape[2]
        across = (width, cells_h + 2 * width, channels, 128)
        along = (cells_d + 2 * width, width, channels, 128)

        @pl.when(d == 0)
        def _():
            buf[0:width] = jnp.zeros(across, BF16)

        @pl.when(d == ND - 1)
        def _():
            buf[cells_d + width : cells_d + 2 * width] = jnp.zeros(across, BF16)

        @pl.when(h == 0)
        def _():
            buf[:, 0:width] = jnp.zeros(along, BF16)

        @pl.when(h == NH - 1)
        def _():
            buf[:, cells_h + width : cells_h + 2 * width] = jnp.zeros(along, BF16)

    def scatter_h(src, dst, send, recv, k):
        other = lax.rem(h + k, NH)
        return pltpu.make_async_remote_copy(
            src_ref=src.at[other],
            dst_ref=dst.at[k],
            send_sem=send.at[k],
            recv_sem=recv.at[k],
            device_id=partner(other),
            device_id_type=MESH,
        )

    def share_d(src, dst, send, recv, k):
        return pltpu.make_async_remote_copy(
            src_ref=src,
            dst_ref=dst.at[k],
            send_sem=send.at[k],
            recv_sem=recv.at[k],
            device_id=around(k, 0),
            device_id_type=MESH,
        )

    def gather_send(src, dst, send, recv, k):
        return pltpu.make_async_remote_copy(
            src_ref=src,
            dst_ref=dst.at[h],
            send_sem=send.at[k],
            recv_sem=recv.at[k],
            device_id=partner(lax.rem(h + k, NH)),
            device_id_type=MESH,
        )

    def gather_recv(src, dst, send, recv, k):
        return pltpu.make_async_remote_copy(
            src_ref=src,
            dst_ref=dst.at[lax.rem(h - k + NH, NH)],
            send_sem=send.at[k],
            recv_sem=recv.at[k],
            device_id=partner(lax.rem(h + k, NH)),
            device_id_type=MESH,
        )

    halo_x = (0, xb, 4, 8, 1)
    halo_p = (1, pk, 2, 4, 2)
    halo_c = (2, ck, 2, 4, 1)
    halo_d3 = (3, d3, 4, 8, 1)
    halo_start(*halo_x)
    each(1, NH, lambda k: gather_send(f4, bank, ag_s, ag_r, k).start())
    bank[h] = f4[...]

    def stack_x(i):
        for j in range(10):
            xx[i, j] = stack_width(xb[i, j], 1)

    halo_wait(*halo_x)
    halo_start(*halo_c)
    stage("stack_x", lambda: each(0, 6, stack_x))

    def forward3(i):
        for j in range(4):
            total = None
            for di in range(2):
                cols = [
                    jnp.concatenate(
                        [xx[2 * i + di + a, 2 * j + s + b] for a in range(3) for b in range(3)],
                        axis=0,
                    )
                    for s in range(2)
                ]
                act = jnp.dot(
                    a3[...], jnp.concatenate(cols, axis=1), preferred_element_type=F32
                )
                value, slope = gelu_parts(act)
                for s in range(2):
                    slope3[2 * i + di, 2 * j + s] = slope[:, 128 * s : 128 * s + 128]
                both = value[:, :128] + value[:, 128:]
                total = both if total is None else total + both
            total = (total + pltpu.roll(total, 127, 1)) * 0.125
            pk[2 + i, 2 + j] = interleave(total[:32], total[32:]).astype(BF16)

    stage("forward3", lambda: each(0, 2, forward3))
    halo_start(*halo_p)

    def wait_gather(k):
        gather_send(f4, bank, ag_s, ag_r, k).wait_send()
        gather_recv(f4, bank, ag_s, ag_r, k).wait_recv()

    each(1, NH, wait_gather)

    def arrange():
        wide = [bank[s].astype(F32) for s in range(NH)]
        low = jnp.concatenate([w[:8] for w in wide], axis=0)
        high = jnp.concatenate([w[8:] for w in wide], axis=0)
        a4[...] = jnp.concatenate([low, high], axis=1).astype(BF16)
        for ab in range(9):
            a5[:, 128 * ab : 128 * ab + 128] = jnp.transpose(
                a4[:, 192 * ab : 192 * ab + 192].astype(F32)
            ).astype(BF16)

    stage("arrange", arrange)
    halo_wait(*halo_c)
    halo_wait(*halo_p)

    def stack_p(i):
        for j in range(8):
            both = two_rows(pk[i, j].astype(F32), pk[i + 2, j].astype(F32))
            before, after = shifted(both, 2)
            pq[i, j] = jnp.concatenate([before, both, after], axis=0).astype(BF16)

    stage("stack_p", lambda: each(0, 4, stack_p))

    def forward4(i):
        for j in range(3):
            cols = [
                jnp.concatenate(
                    [pq[i + a, 2 * j + s + b] for a in range(3) for b in range(3)], axis=0
                )
                for s in range(2)
            ]
            act = jnp.dot(
                a4[:, :1728], jnp.concatenate(cols, axis=1), preferred_element_type=F32
            )
            _, slope = gelu_parts(act)
            for s in range(2):
                col = 2 * j + s
                both = two_rows(ck[i, col].astype(F32), ck[i + 2, col].astype(F32))
                dq[i, col] = (both * slope[:, 128 * s : 128 * s + 128]).astype(BF16)

    stage("forward4", lambda: each(0, 2, forward4))

    def pair_rows():
        for j in range(6):
            one, two = dq[0, j].astype(F32), dq[1, j].astype(F32)
            even = lanes_iota(one.shape) % 2 == 0
            dv[0, j] = interleave_odd(one, two).astype(BF16)
            dv[1, j] = jnp.where(even, two, one).astype(BF16)
            dv[2, j] = interleave(one, two).astype(BF16)

    stage("pair_rows", pair_rows)

    def back4(j):
        cols = [
            jnp.concatenate([dv[a, 2 * j + s + 2 - b] for a in range(3) for b in range(3)], axis=0)
            for s in range(2)
        ]
        y = jnp.dot(a5[...], jnp.concatenate(cols, axis=1), preferred_element_type=F32)
        for s in range(2):
            ys = y[:, 128 * s : 128 * s + 128]
            _, from_after = shifted(ys[:64], 2)
            from_before, _ = shifted(ys[128:], 2)
            back = (ys[64:128] + from_after + from_before) * 0.125
            even = lanes_iota(back.shape) % 2 == 0
            spread = [
                jnp.where(even, back, pltpu.roll(back, 1, 1)),
                jnp.where(even, pltpu.roll(back, 127, 1), back),
            ]
            for i in range(2):
                for di in range(2):
                    for dj in range(2):
                        row, col = 2 * i + di, 2 * (2 * j + s) + dj
                        d3[1 + row, 1 + col] = (spread[i] * slope3[row, col]).astype(BF16)

    stage("back4", lambda: each(0, 2, back4))
    halo_start(*halo_d3)

    f3acc[...] = jnp.zeros(f3acc.shape, F32)

    def weight3(i):
        left = jnp.concatenate([d3[1 + i, 1 + j] for j in range(8)], axis=1)
        right = jnp.concatenate(
            [
                jnp.concatenate([xx[i + a, j + b] for j in range(8)], axis=1)
                for a in range(3)
                for b in range(3)
            ],
            axis=0,
        )
        f3acc[:, :864] += lax.dot_general(
            left, right, (((1,), (1,)), ((), ())), preferred_element_type=F32
        )

    stage("weight3", lambda: each(0, 4, weight3))

    def pack3():
        for c in range(16):
            r3[c] = f3acc[
                16 * (c % 4) : 16 * (c % 4) + 16, 256 * (c // 4) : 256 * (c // 4) + 256
            ].astype(BF16)

    stage("pack3", pack3)
    each(1, NH, lambda k: scatter_h(r3, q3, s3_s, s3_r, k).start())

    cells4 = [(i, j) for i in range(2) for j in range(4)]

    def weight4():
        even = lanes_iota((128, 128)) % 2 == 0
        left = jnp.concatenate(
            [
                jnp.where(even if i == 0 else ~even, dq[1 - i, 1 + j].astype(F32), 0.0)
                for i, j in cells4
            ],
            axis=1,
        ).astype(BF16)
        for g in range(5):
            taps = [ab for ab in (2 * g, 2 * g + 1) if ab < 9]
            right = jnp.concatenate(
                [
                    jnp.concatenate(
                        [pq[ab // 3 + 1 - i, j + ab % 3 + 1] for i, j in cells4], axis=1
                    )
                    for ab in taps
                ],
                axis=0,
            )
            piece = lax.dot_general(
                left, right, (((1,), (1,)), ((), ())), preferred_element_type=F32
            )
            if len(taps) == 1:
                piece = jnp.concatenate([piece, jnp.zeros((128, 64), F32)], axis=1)
            f4acc[:, 384 * g : 384 * g + piece.shape[1]] = piece

    stage("weight4", weight4)

    def pack4(s):
        rows = pl.ds(pl.multiple_of(8 * s, 8), 8)
        r4[s] = jnp.concatenate([f4acc[rows, :896], f4acc[rows, 896:]], axis=0).astype(BF16)

    stage("pack4", lambda: each(0, NH, pack4))
    each(1, NH, lambda k: scatter_h(r4, q4, s4_s, s4_r, k).start())

    def wait_both(copy):
        copy.wait_send()
        copy.wait_recv()

    each(1, NH, lambda k: wait_both(scatter_h(r3, q3, s3_s, s3_r, k)))

    def sum3():
        total3 = r3[h].astype(F32)
        for k in range(1, NH):
            total3 = total3 + q3[k].astype(F32)
        t3[...] = total3

    stage("sum3", sum3)
    each(1, ND, lambda k: share_d(t3, q3b, b3_s, b3_r, k).start())

    halo_wait(*halo_d3)

    def back3(i):
        for j in range(4):
            cols = [
                jnp.concatenate(
                    [d3[i + 2 - a, 2 * j + s + 2 - b] for a in range(3) for b in range(3)], axis=0
                )
                for s in range(2)
            ]
            y = jnp.dot(a6[...], jnp.concatenate(cols, axis=1), preferred_element_type=F32)
            for s in range(2):
                ys = y[:, 128 * s : 128 * s + 128]
                _, from_after = shifted(ys[:32], 1)
                from_before, _ = shifted(ys[64:], 1)
                gv_out[i, 2 * j + s] = (ys[32:64] + from_after + from_before).astype(BF16)

    stage("back3", lambda: each(0, 4, back3))

    each(1, NH, lambda k: wait_both(scatter_h(r4, q4, s4_s, s4_r, k)))

    def sum4():
        total4 = r4[h].astype(F32)
        for k in range(1, NH):
            total4 = total4 + q4[k].astype(F32)
        t4[...] = total4.astype(BF16)

    stage("sum4", sum4)
    each(1, ND, lambda k: share_d(t4, q4b, b4_s, b4_r, k).start())

    each(1, ND, lambda k: wait_both(share_d(t3, q3b, b3_s, b3_r, k)))
    whole3 = t3[...]
    for k in range(1, ND):
        whole3 = whole3 + q3b[k]
    v3[h] = (whole3 * (1.0 / math.sqrt(32 * 128 * 128))).astype(BF16)
    each(1, NH, lambda k: gather_send(v3.at[h], v3, c3_s, c3_r, k).start())

    each(1, ND, lambda k: wait_both(share_d(t4, q4b, b4_s, b4_r, k)))
    whole4 = t4[...].astype(F32)
    for k in range(1, ND):
        whole4 = whole4 + q4b[k].astype(F32)
    g4_out[...] = whole4 * (1.0 / math.sqrt(16 * 64 * 64))

    def wait_c3(k):
        gather_send(v3.at[h], v3, c3_s, c3_r, k).wait_send()
        gather_recv(v3.at[h], v3, c3_s, c3_r, k).wait_recv()

    each(1, NH, wait_c3)
    for c in range(16):
        g3_out[16 * (c % 4) : 16 * (c % 4) + 16, 256 * (c // 4) : 256 * (c // 4) + 256] = v3[
            c
        ].astype(F32)


def shards(volume, filters_three, filters_four, cotangent):
    x_in = jnp.transpose(volume, (1, 2, 0, 3))
    a3 = jnp.transpose(filters_three, (1, 0, 2)).reshape(64, 864)
    a6 = jnp.transpose(filters_three.reshape(9, 3, 64, 32), (1, 3, 0, 2)).reshape(96, 576)
    f4 = jnp.pad(jnp.transpose(filters_four, (1, 0, 2)).reshape(8, 1728), ((0, 0), (0, 64)))
    f4 = jnp.transpose(f4.reshape(8, 2, 896), (1, 0, 2)).reshape(16, 896)
    cot = jnp.transpose(cotangent, (1, 2, 0, 3))

    vmem = pl.BlockSpec(memory_space=pltpu.VMEM)
    dma = pltpu.SemaphoreType.DMA
    gv, g3, g4 = pl.pallas_call(
        kernel,
        out_shape=(
            jax.ShapeDtypeStruct((4, 8, 32, 128), BF16),
            jax.ShapeDtypeStruct((64, 1024), F32),
            jax.ShapeDtypeStruct((16, 896), F32),
        ),
        in_specs=[vmem] * 5,
        out_specs=(vmem,) * 3,
        scratch_shapes=[
            pltpu.VMEM((6, 10, 32, 128), BF16),
            pltpu.VMEM((6, 10, 96, 128), BF16),
            pltpu.VMEM((4, 8, 64, 128), F32),
            pltpu.VMEM((4, 6, 64, 128), BF16),
            pltpu.VMEM((6, 8, 32, 128), BF16),
            pltpu.VMEM((4, 8, 192, 128), BF16),
            pltpu.VMEM((2, 6, 128, 128), BF16),
            pltpu.VMEM((3, 6, 128, 128), BF16),
            pltpu.VMEM((6, 10, 64, 128), BF16),
            pltpu.VMEM((16, 16, 896), BF16),
            pltpu.VMEM((128, 1792), BF16),
            pltpu.VMEM((192, 1152), BF16),
            pltpu.VMEM((128, 1792), F32),
            pltpu.VMEM((16, 16, 896), BF16),
            pltpu.VMEM((16, 16, 896), BF16),
            pltpu.VMEM((16, 896), BF16),
            pltpu.VMEM((8, 16, 896), BF16),
            pltpu.VMEM((64, 1024), F32),
            pltpu.VMEM((16, 16, 256), BF16),
            pltpu.VMEM((16, 16, 256), BF16),
            pltpu.VMEM((16, 256), F32),
            pltpu.VMEM((8, 16, 256), F32),
            pltpu.VMEM((16, 16, 256), BF16),
            dma((4, 8)),
            dma((4, 8)),
            dma((16,)),
            dma((16,)),
            dma((16,)),
            dma((16,)),
            dma((8,)),
            dma((8,)),
            dma((16,)),
            dma((16,)),
            dma((8,)),
            dma((8,)),
            dma((16,)),
            dma((16,)),
        ],
        compiler_params=pltpu.CompilerParams(
            collective_id=0, has_side_effects=True, vmem_limit_bytes=40 * 1024 * 1024
        ),
    )(x_in, a3, a6, f4, cot)

    grad_volume = jnp.transpose(gv, (2, 0, 1, 3))
    grad_three = jnp.transpose(g3[:, :864].reshape(64, 27, 32), (1, 0, 2))
    g4 = jnp.transpose(g4.reshape(2, 8, 896), (1, 0, 2)).reshape(8, 1792)
    grad_four = jnp.transpose(g4[:, :1728].reshape(8, 27, 64), (1, 0, 2))
    return (grad_volume, grad_three, grad_four)


def solution(mesh):
    in_specs = (
        P(None, "depth", "height", None),
        P(),
        P(None, "height", None),
        P(None, "depth", "height", None),
    )
    out_specs = (P(None, "depth", "height", None), P(), P(None, "height", None))
    return jax.shard_map(shards, mesh=mesh, in_specs=in_specs, out_specs=out_specs, check_vma=False)
```

time: 80.5 us -> 58 us (0.72)
  Pallas kernels: 68.9 us -> 51.3 us
  local copies, waits for them, and re-layouts: 10.8 us -> 5.85 us
    pallas_call x1, Pallas kernels: 68.9 us -> 51.3 us  [shards(): pl.pallas_call(kernel, out_shape=(jax.ShapeDtypeStruct((4, 8, 32, 128), B...]
    pad x1 -> x0, local copies, waits for them, and re-layouts: 4.92 us -> none  [shards(): lax.pad(cot, jnp.zeros((), BF16), ((0, 0, 0), (0, 0, 0), (0, 0, 0), (0, 1...]
where the time goes in v2:
time: 58 us; the launch traced here: 57.8 us
  Pallas kernels  51.3 us (88%)
  local copies, waits for them, and re-layouts  5.85 us (10%)
  between operations  0.69 us (1%)
    pallas_call x1, Pallas kernels, shards(): pl.pallas_call(kernel, out_shape=(jax.ShapeDtypeStruct((4, 8, 32, 128), B...  51.3 us
    unnamed x10, local copies, waits for them, and re-layouts  3.28 us

profile of v2, /device:TPU:1, one launch (start us, length us, event | category | flops | bytes accessed | tf_op | source)
XLA Modules:
  0.0 57.8 jit_solution(12857895595892740679)
XLA Ops:
  0.6 0.0 copy-start
  0.6 0.9 %copy.15 = bf16[8,27,64]{2,1,0:T(8,128)(2,1)S(1)} copy(bf16[8,27,64]{2,0,1:T(8,128)(2,1)} %bitcast.38) | data formatting | bytes 55296 | tf_op jit(solution)/shard_map/transpose | solution.py:470
  1.5 0.0 copy-start.1
  1.5 0.1 reshape.39
  1.7 0.0 copy-done
  1.7 0.1 copy.17.a3
  1.8 0.7 %copy-done.1 = bf16[32,4,8,128]{3,2,1,0:T(8,128)(2,1)S(1)} copy-done((bf16[32,4,8,128]{3,2,1,0:T(8,128)(2,1)S(1)}, bf16[32,4,8,128]{3,2,1,0:T(8,128)(2,1)}, u32[]{:S(2)}) %copy-start.1) | copy-done | bytes 262168
  2.5 0.0 copy-start.2
  2.5 0.1 copy.24
  2.6 0.8 %copy-done.2 = bf16[128,2,4,64]{0,3,2,1:T(8,128)(2,1)S(1)} copy-done((bf16[128,2,4,64]{0,3,2,1:T(8,128)(2,1)S(1)}, bf16[128,2,4,64]{0,3,2,1:T(8,128)(2,1)}, u32[]{:S(2)}) %copy-start.2) | copy-done | bytes 131096
  3.4 0.2 copy.16
  3.6 0.1 copy.23
  3.7 0.2 reshape.38.a6
  3.9 51.3 %shard_map.67 = (bf16[4,8,32,128]{3,2,1,0:T(8,128)(2,1)S(1)}, f32[64,1024]{1,0:T(8,128)S(1)}, f32[16,896]{1,0:T(8,128)S(1)}) custom-call(bf16[4,8,32,128]{3,2,1,0:T(8,128)(2,1)S(1)} %bitcast.28, bf16[64,864]{1,0:T(8,128)(2,1)S(1)} %copy.17.a3, bf16[96,576]{1,0:T(8,128)(2,1)S(1)} %reshape.38.a6, bf16[16,896]{1,0:T(8,128)(2,1)S(1)} %bitcast.31, ...), custom_call_target="tpu_custom_call" | custom-call | tf_op jit(solution)/shard_map/pallas_call | solution.py:476
  55.3 0.8 %copy.19 = bf16[32,4,8,128]{3,2,1,0:T(8,128)(2,1)} copy(bf16[32,4,8,128]{3,0,2,1:T(8,128)(2,1)S(1)} %bitcast.30) | data formatting | bytes 524288
  56.1 0.1 reshape.45
  56.1 0.7 %copy.20 = f32[27,8,64]{2,1,0:T(8,128)} copy(f32[27,8,64]{2,0,1:T(8,128)S(1)} %bitcast.36) | data formatting | bytes 110592
  56.9 1.0 %copy.18 = f32[64,864]{0,1:T(8,128)} copy(f32[64,864]{1,0:T(8,128)S(1)} %slice.6) | data formatting | bytes 442368 | tf_op jit(solution)/shard_map/slice | solution.py:530
  (2 shorter events, 0.0 us)
Async XLA Ops:
  0.6 1.0 %copy-start = (bf16[27,64,32]{1,2,0:T(8,128)(2,1)S(1)}, bf16[27,64,32]{1,2,0:T(8,128)(2,1)}, u32[]{:S(2)}) copy-start(bf16[27,64,32]{1,2,0:T(8,128)(2,1)} %param.5) | copy-start | bytes 331780
  1.5 1.0 %copy-start.1 = (bf16[32,4,8,128]{3,2,1,0:T(8,128)(2,1)S(1)}, bf16[32,4,8,128]{3,2,1,0:T(8,128)(2,1)}, u32[]{:S(2)}) copy-start(bf16[32,4,8,128]{3,2,1,0:T(8,128)(2,1)} %param.4) | copy-start | bytes 786436
  2.5 0.9 %copy-start.2 = (bf16[128,2,4,64]{0,3,2,1:T(8,128)(2,1)S(1)}, bf16[128,2,4,64]{0,3,2,1:T(8,128)(2,1)}, u32[]{:S(2)}) copy-start(bf16[128,2,4,64]{0,3,2,1:T(8,128)(2,1)} %param.7) | copy-start | bytes 393220

commit v3 on v2

--- a/solution.py
+++ b/solution.py
@@ -21,10 +21,10 @@
 
 def gelu_parts(v):
     u = v * v
-    inner = jnp.tanh(TANH_SCALE * (v + CUBIC_TERM * v * u))
-    half = 0.5 * (1.0 + inner)
+    inner = jnp.tanh(v * (TANH_SCALE + TANH_SCALE * CUBIC_TERM * u))
+    half = 0.5 + 0.5 * inner
     value = v * half
-    slope = half + 0.5 * v * (1.0 - inner * inner) * TANH_SCALE * (1.0 + 3.0 * CUBIC_TERM * u)
+    slope = half + value * (1.0 - inner) * (TANH_SCALE + 3.0 * TANH_SCALE * CUBIC_TERM * u)
     return value, slope
 
 
@@ -71,12 +71,13 @@
 
 
 def kernel(
-    x_in, a3, a6, f4, cot,
+    x_hbm, f3_hbm, f4_hbm, cot_hbm,
     gv_out, g3_out, g4_out,
-    xb, xx, slope3, ck, pk, pq, dq, dv, d3, bank, a4, a5,
+    x_in, f3, f4_in, cot, f4, a3, a6,
+    xb, xx, slope3, ck, pk, pq, dq, dv, d3, dd3, bank, a4, a5,
     f4acc, r4, q4, t4, q4b,
     f3acc, r3, q3, t3, q3b, v3,
-    halo_s, halo_r, ag_s, ag_r, s4_s, s4_r, b4_s, b4_r, s3_s, s3_r, b3_s, b3_r, c3_s, c3_r,
+    in_sem, halo_s, halo_r, ag_s, ag_r, s4_s, s4_r, b4_s, b4_r, s3_s, s3_r, b3_s, b3_r, c3_s, c3_r,
 ):
     d = lax.axis_index("depth")
     h = lax.axis_index("height")
@@ -107,21 +108,33 @@
     for k in range(2, ND - 1):
         greet(around(k, 0))
 
-    def dilate():
-        at = 2 * lax.broadcasted_iota(jnp.int32, (64, 128), 0)
-        lane = lanes_iota((64, 128))
-        to_even = (lane == at).astype(F32).astype(BF16)
-        to_odd = (lane == at + 1).astype(F32).astype(BF16)
-        for i in range(2):
-            for j in range(4):
-                row = cot[i, j]
-                ck[1 + i, 1 + j] = (
-                    jnp.dot(row[:64], to_even, preferred_element_type=F32)
-                    + jnp.dot(row[64:], to_odd, preferred_element_type=F32)
-                ).astype(BF16)
-
-    xb[1:5, 1:9] = x_in[...]
-    stage("dilate", dilate)
+    fetches = [
+        pltpu.make_async_copy(src, dst, in_sem.at[n])
+        for n, (src, dst) in enumerate(
+            [(x_hbm, x_in), (f4_hbm, f4_in), (f3_hbm, f3), (cot_hbm, cot)]
+        )
+    ]
+    for fetch in fetches:
+        fetch.start()
+
+    def rows_x():
+        for i in range(4):
+            block = jnp.transpose(x_in[:, i].astype(F32), (1, 0, 2)).astype(BF16)
+            for j in range(8):
+                xb[1 + i, 1 + j] = block[j]
+
+    fetches[0].wait()
+    stage("rows_x", rows_x)
+
+    def rows_f4():
+        taps = [f4_in[t].astype(F32) for t in range(27)] + [jnp.zeros((8, 64), F32)]
+        tiles = [jnp.concatenate([taps[2 * m], taps[2 * m + 1]], axis=1) for m in range(14)]
+        f4[...] = jnp.concatenate(
+            [jnp.concatenate(tiles[:7], axis=1), jnp.concatenate(tiles[7:], axis=1)], axis=0
+        ).astype(BF16)
+
+    fetches[1].wait()
+    stage("rows_f4", rows_f4)
     pl.semaphore_wait(barrier, 8 + NH - 1 + ND - 3)
 
     def halo_copy(which, n, buf, cells_d, cells_h, width):
@@ -214,33 +227,69 @@
     each(1, NH, lambda k: gather_send(f4, bank, ag_s, ag_r, k).start())
     bank[h] = f4[...]
 
+    def dilate():
+        at = 2 * lax.broadcasted_iota(jnp.int32, (64, 128), 0)
+        to_even = (lanes_iota((64, 128)) == at).astype(F32).astype(BF16)
+        for i in range(2):
+            for j in range(4):
+                wide = lax.dot_general(
+                    cot[i, j], to_even, (((0,), (0,)), ((), ())), preferred_element_type=F32
+                )
+                ck[1 + i, 1 + j] = interleave(wide[:64], wide[64:]).astype(BF16)
+
+    def rows_f3():
+        flat = f3[...].astype(F32).reshape(864, 64)
+        none = jnp.zeros((288, 64), F32)
+        both = jnp.concatenate(
+            [jnp.concatenate([flat, none], axis=0), jnp.concatenate([none, flat], axis=0)], axis=1
+        )
+        a3[...] = jnp.transpose(both).astype(BF16)
+        a6[...] = jnp.concatenate(
+            [flat[96 * ab : 96 * ab + 96] for ab in range(9)], axis=1
+        ).astype(BF16)
+
+    def stack_row(i, j):
+        xx[i, j] = stack_width(xb[i, j], 1)
+
     def stack_x(i):
-        for j in range(10):
-            xx[i, j] = stack_width(xb[i, j], 1)
-
+        for j in range(8):
+            stack_row(1 + i, 1 + j)
+
+    fetches[2].wait()
+    stage("rows_f3", rows_f3)
+    fetches[3].wait()
+    stage("dilate", dilate)
+    stage("stack_x", lambda: each(0, 4, stack_x))
     halo_wait(*halo_x)
     halo_start(*halo_c)
-    stage("stack_x", lambda: each(0, 6, stack_x))
+
+    def stack_rim():
+        for j in range(10):
+            stack_row(0, j)
+            stack_row(5, j)
+        for i in range(4):
+            stack_row(1 + i, 0)
+            stack_row(1 + i, 9)
+
+    stage("stack_rim", stack_rim)
 
     def forward3(i):
         for j in range(4):
-            total = None
+            cols = [
+                jnp.concatenate(
+                    [xx[2 * i + a, 2 * j + s + b] for a in range(4) for b in range(3)], axis=0
+                )
+                for s in range(2)
+            ]
+            act = jnp.dot(a3[...], jnp.concatenate(cols, axis=1), preferred_element_type=F32)
+            value, slope = gelu_parts(act)
             for di in range(2):
-                cols = [
-                    jnp.concatenate(
-                        [xx[2 * i + di + a, 2 * j + s + b] for a in range(3) for b in range(3)],
-                        axis=0,
-                    )
-                    for s in range(2)
-                ]
-                act = jnp.dot(
-                    a3[...], jnp.concatenate(cols, axis=1), preferred_element_type=F32
-                )
-                value, slope = gelu_parts(act)
                 for s in range(2):
-                    slope3[2 * i + di, 2 * j + s] = slope[:, 128 * s : 128 * s + 128]
-                both = value[:, :128] + value[:, 128:]
-                total = both if total is None else total + both
+                    slope3[2 * i + di, 2 * j + s] = slope[
+                        64 * di : 64 * di + 64, 128 * s : 128 * s + 128
+                    ]
+            total = value[:64] + value[64:]
+            total = total[:, :128] + total[:, 128:]
             total = (total + pltpu.roll(total, 127, 1)) * 0.125
             pk[2 + i, 2 + j] = interleave(total[:32], total[32:]).astype(BF16)
 
@@ -324,7 +373,11 @@
                 for di in range(2):
                     for dj in range(2):
                         row, col = 2 * i + di, 2 * (2 * j + s) + dj
-                        d3[1 + row, 1 + col] = (spread[i] * slope3[row, col]).astype(BF16)
+                        delta = spread[i] * slope3[row, col]
+                        before, after = shifted(delta, 1)
+                        stack = jnp.concatenate([after, delta, before], axis=0).astype(BF16)
+                        dd3[row, col] = stack
+                        d3[1 + row, 1 + col] = stack[64:128]
 
     stage("back4", lambda: each(0, 2, back4))
     halo_start(*halo_d3)
@@ -332,26 +385,33 @@
     f3acc[...] = jnp.zeros(f3acc.shape, F32)
 
     def weight3(i):
-        left = jnp.concatenate([d3[1 + i, 1 + j] for j in range(8)], axis=1)
-        right = jnp.concatenate(
+        left = jnp.concatenate(
             [
-                jnp.concatenate([xx[i + a, j + b] for j in range(8)], axis=1)
+                jnp.concatenate([xb[i + a, j + b] for j in range(8)], axis=1)
                 for a in range(3)
                 for b in range(3)
             ],
             axis=0,
         )
-        f3acc[:, :864] += lax.dot_general(
+        right = jnp.concatenate([dd3[i, j] for j in range(8)], axis=1)
+        f3acc[...] += lax.dot_general(
             left, right, (((1,), (1,)), ((), ())), preferred_element_type=F32
         )
 
     stage("weight3", lambda: each(0, 4, weight3))
 
     def pack3():
+        last = f3acc[:, 128:]
+        flat = jnp.concatenate(
+            [
+                f3acc[:, :128],
+                jnp.concatenate([last[:144], last[144:]], axis=1),
+                jnp.zeros((80, 128), F32),
+            ],
+            axis=0,
+        ).astype(BF16)
         for c in range(16):
-            r3[c] = f3acc[
-                16 * (c % 4) : 16 * (c % 4) + 16, 256 * (c // 4) : 256 * (c // 4) + 256
-            ].astype(BF16)
+            r3[c] = flat[32 * c : 32 * c + 32]
 
     stage("pack3", pack3)
     each(1, NH, lambda k: scatter_h(r3, q3, s3_s, s3_r, k).start())
@@ -412,6 +472,7 @@
     halo_wait(*halo_d3)
 
     def back3(i):
+        done = []
         for j in range(4):
             cols = [
                 jnp.concatenate(
@@ -424,7 +485,8 @@
                 ys = y[:, 128 * s : 128 * s + 128]
                 _, from_after = shifted(ys[:32], 1)
                 from_before, _ = shifted(ys[64:], 1)
-                gv_out[i, 2 * j + s] = (ys[32:64] + from_after + from_before).astype(BF16)
+                done.append(ys[32:64] + from_after + from_before)
+        gv_out[:, i] = jnp.transpose(jnp.stack(done, axis=0), (1, 0, 2)).astype(BF16)
 
     stage("back3", lambda: each(0, 4, back3))
 
@@ -450,39 +512,46 @@
     whole4 = t4[...].astype(F32)
     for k in range(1, ND):
         whole4 = whole4 + q4b[k].astype(F32)
-    g4_out[...] = whole4 * (1.0 / math.sqrt(16 * 64 * 64))
+    whole4 = whole4 * (1.0 / math.sqrt(16 * 64 * 64))
+    for t in range(27):
+        rows, lane = 8 * (t // 14), 64 * (t % 14)
+        g4_out[t] = whole4[rows : rows + 8, lane : lane + 64]
 
     def wait_c3(k):
         gather_send(v3.at[h], v3, c3_s, c3_r, k).wait_send()
         gather_recv(v3.at[h], v3, c3_s, c3_r, k).wait_recv()
 
     each(1, NH, wait_c3)
-    for c in range(16):
-        g3_out[16 * (c % 4) : 16 * (c % 4) + 16, 256 * (c // 4) : 256 * (c // 4) + 256] = v3[
-            c
-        ].astype(F32)
+    flat3 = jnp.concatenate([v3[c].astype(F32) for c in range(14)], axis=0)
+    last3 = jnp.concatenate([flat3[288:432, :64], flat3[288:432, 64:]], axis=0)
+    for ab in range(9):
+        rows = slice(32 * ab, 32 * ab + 32)
+        g3_out[3 * ab] = flat3[rows, :64]
+        g3_out[3 * ab + 1] = flat3[rows, 64:]
+        g3_out[3 * ab + 2] = last3[rows]
 
 
 def shards(volume, filters_three, filters_four, cotangent):
-    x_in = jnp.transpose(volume, (1, 2, 0, 3))
-    a3 = jnp.transpose(filters_three, (1, 0, 2)).reshape(64, 864)
-    a6 = jnp.transpose(filters_three.reshape(9, 3, 64, 32), (1, 3, 0, 2)).reshape(96, 576)
-    f4 = jnp.pad(jnp.transpose(filters_four, (1, 0, 2)).reshape(8, 1728), ((0, 0), (0, 64)))
-    f4 = jnp.transpose(f4.reshape(8, 2, 896), (1, 0, 2)).reshape(16, 896)
-    cot = jnp.transpose(cotangent, (1, 2, 0, 3))
-
     vmem = pl.BlockSpec(memory_space=pltpu.VMEM)
+    hbm = pl.BlockSpec(memory_space=pl.ANY)
     dma = pltpu.SemaphoreType.DMA
     gv, g3, g4 = pl.pallas_call(
         kernel,
         out_shape=(
-            jax.ShapeDtypeStruct((4, 8, 32, 128), BF16),
-            jax.ShapeDtypeStruct((64, 1024), F32),
-            jax.ShapeDtypeStruct((16, 896), F32),
+            jax.ShapeDtypeStruct((32, 4, 8, 128), BF16),
+            jax.ShapeDtypeStruct((27, 32, 64), F32),
+            jax.ShapeDtypeStruct((27, 8, 64), F32),
         ),
-        in_specs=[vmem] * 5,
+        in_specs=[hbm] * 4,
         out_specs=(vmem,) * 3,
         scratch_shapes=[
+            pltpu.VMEM((32, 4, 8, 128), BF16),
+            pltpu.VMEM((27, 32, 64), BF16),
+            pltpu.VMEM((27, 8, 64), BF16),
+            pltpu.VMEM((2, 4, 64, 128), BF16),
+            pltpu.VMEM((16, 896), BF16),
+            pltpu.VMEM((128, 1152), BF16),
+            pltpu.VMEM((96, 576), BF16),
             pltpu.VMEM((6, 10, 32, 128), BF16),
             pltpu.VMEM((6, 10, 96, 128), BF16),
             pltpu.VMEM((4, 8, 64, 128), F32),
@@ -492,6 +561,7 @@
             pltpu.VMEM((2, 6, 128, 128), BF16),
             pltpu.VMEM((3, 6, 128, 128), BF16),
             pltpu.VMEM((6, 10, 64, 128), BF16),
+            pltpu.VMEM((4, 8, 192, 128), BF16),
             pltpu.VMEM((16, 16, 896), BF16),
             pltpu.VMEM((128, 1792), BF16),
             pltpu.VMEM((192, 1152), BF16),
@@ -500,12 +570,13 @@
             pltpu.VMEM((16, 16, 896), BF16),
             pltpu.VMEM((16, 896), BF16),
             pltpu.VMEM((8, 16, 896), BF16),
-            pltpu.VMEM((64, 1024), F32),
-            pltpu.VMEM((16, 16, 256), BF16),
-            pltpu.VMEM((16, 16, 256), BF16),
-            pltpu.VMEM((16, 256), F32),
-            pltpu.VMEM((8, 16, 256), F32),
-            pltpu.VMEM((16, 16, 256), BF16),
+            pltpu.VMEM((288, 192), F32),
+            pltpu.VMEM((16, 32, 128), BF16),
+            pltpu.VMEM((16, 32, 128), BF16),
+            pltpu.VMEM((32, 128), F32),
+            pltpu.VMEM((8, 32, 128), F32),
+            pltpu.VMEM((16, 32, 128), BF16),
+            dma((4,)),
             dma((4, 8)),
             dma((4, 8)),
             dma((16,)),
@@ -524,13 +595,13 @@
         compiler_params=pltpu.CompilerParams(
             collective_id=0, has_side_effects=True, vmem_limit_bytes=40 * 1024 * 1024
         ),
-    )(x_in, a3, a6, f4, cot)
-
-    grad_volume = jnp.transpose(gv, (2, 0, 1, 3))
-    grad_three = jnp.transpose(g3[:, :864].reshape(64, 27, 32), (1, 0, 2))
-    g4 = jnp.transpose(g4.reshape(2, 8, 896), (1, 0, 2)).reshape(8, 1792)
-    grad_four = jnp.transpose(g4[:, :1728].reshape(8, 27, 64), (1, 0, 2))
-    return (grad_volume, grad_three, grad_four)
+    )(
+        volume,
+        jnp.transpose(filters_three, (0, 2, 1)),
+        filters_four,
+        jnp.transpose(cotangent, (1, 2, 3, 0)),
+    )
+    return (gv, jnp.transpose(g3, (0, 2, 1)), g4)
 
 
 def solution(mesh):

time: 58 us -> 56.9 us (0.981)
  Pallas kernels: 51.3 us -> 50.3 us
    unnamed x10 -> x11, local copies, waits for them, and re-layouts: 3.28 us -> 5.71 us
    pallas_call x1, Pallas kernels: 51.3 us -> 50.3 us  [shards(): pl.pallas_call(kernel, out_shape=(jax.ShapeDtypeStruct((32, 4, 8, 128), B...]
    slice x2 -> x0, local copies, waits for them, and re-layouts: 0.98 us -> none  [shards(): grad_three = jnp.transpose(g3[:, :864].reshape(64, 27, 32), (1, 0, 2))]
    transpose x1 -> x0, local copies, waits for them, and re-layouts: 0.87 us -> none  [shards(): jnp.transpose(filters_four, (1, 0, 2)).reshape(8, 1728)]
    reshape x5 -> x0, local copies, waits for them, and re-layouts: 0.72 us -> none  [the longest x1 0.25 us: shards(): jnp.transpose(filters_three.reshape(9, 3, 64, 32), (1, 3, 0, 2))]
where the time goes in v3:
time: 56.9 us; the launch traced here: 56.7 us
  Pallas kernels  50.3 us (88%)
  local copies, waits for them, and re-layouts  5.71 us (10%)
  between operations  0.65 us (1%)
    pallas_call x1, Pallas kernels, shards(): pl.pallas_call(kernel, out_shape=(jax.ShapeDtypeStruct((32, 4, 8, 128), B...  50.3 us
    unnamed x11, local copies, waits for them, and re-layouts  5.71 us

profile of v3, /device:TPU:1, one launch (start us, length us, event | category | flops | bytes accessed | tf_op | source)
XLA Modules:
  0.0 56.7 jit_solution(1183314848441470284)
XLA Ops:
  0.6 0.0 copy-start
  0.6 0.9 %copy-done = bf16[32,4,8,128]{3,2,1,0:T(8,128)(2,1)S(1)} copy-done((bf16[32,4,8,128]{3,2,1,0:T(8,128)(2,1)S(1)}, bf16[32,4,8,128]{3,2,1,0:T(8,128)(2,1)}, u32[]{:S(2)}) %copy-start) | copy-done | bytes 262168
  1.6 0.0 copy-start.1
  1.6 0.9 %copy-done.1 = bf16[27,64,32]{1,2,0:T(8,128)(2,1)S(1)} copy-done((bf16[27,64,32]{1,2,0:T(8,128)(2,1)S(1)}, bf16[27,64,32]{1,2,0:T(8,128)(2,1)}, u32[]{:S(2)}) %copy-start.1) | copy-done | bytes 110616
  2.5 0.0 copy-start.2
  2.5 0.9 %copy-done.2 = bf16[128,2,4,64]{0,3,2,1:T(8,128)(2,1)S(1)} copy-done((bf16[128,2,4,64]{0,3,2,1:T(8,128)(2,1)S(1)}, bf16[128,2,4,64]{0,3,2,1:T(8,128)(2,1)}, u32[]{:S(2)}) %copy-start.2) | copy-done | bytes 131096
  3.4 0.0 copy-start.3
  3.4 0.8 %copy-done.3 = bf16[27,8,64]{2,1,0:T(8,128)(2,1)S(1)} copy-done((bf16[27,8,64]{2,1,0:T(8,128)(2,1)S(1)}, bf16[27,8,64]{2,1,0:T(8,128)(2,1)}, u32[]{:S(2)}) %copy-start.3) | copy-done | bytes 27672
  4.2 50.3 %shard_map.67 = (bf16[32,4,8,128]{3,2,1,0:T(8,128)(2,1)S(1)}, f32[27,32,64]{2,1,0:T(8,128)S(1)}, f32[27,8,64]{2,1,0:T(8,128)S(1)}) custom-call(bf16[32,4,8,128]{3,2,1,0:T(8,128)(2,1)S(1)} %copy-done, bf16[27,32,64]{2,1,0:T(8,128)(2,1)S(1)} %bitcast.4, bf16[27,8,64]{2,1,0:T(8,128)(2,1)S(1)} %copy-done.3, bf16[2,4,64,128]{3,2,1,0:T(8,128)(2,1)S(1)} %bitcast.5), custom_call_target="tpu_custom_call" | custom-call | tf_op jit(solution)/shard_map/pallas_call | solution.py:538
  54.6 0.7 %copy.10 = bf16[32,4,8,128]{3,2,1,0:T(8,128)(2,1)} copy(bf16[32,4,8,128]{3,2,1,0:T(8,128)(2,1)S(1)} %get-tuple-element.12) | data formatting | bytes 524288
  55.3 0.8 %copy.11 = f32[27,64,32]{1,2,0:T(8,128)} copy(f32[27,64,32]{1,2,0:T(8,128)S(1)} %bitcast.3) | data formatting | bytes 442368
  56.0 0.6 %copy.12 = f32[27,8,64]{2,1,0:T(8,128)} copy(f32[27,8,64]{2,1,0:T(8,128)S(1)} %get-tuple-element.14) | data formatting | bytes 110592
Async XLA Ops:
  0.6 1.0 %copy-start = (bf16[32,4,8,128]{3,2,1,0:T(8,128)(2,1)S(1)}, bf16[32,4,8,128]{3,2,1,0:T(8,128)(2,1)}, u32[]{:S(2)}) copy-start(bf16[32,4,8,128]{3,2,1,0:T(8,128)(2,1)} %x_hbm.1) | copy-start | bytes 786436
  1.6 0.9 %copy-start.1 = (bf16[27,64,32]{1,2,0:T(8,128)(2,1)S(1)}, bf16[27,64,32]{1,2,0:T(8,128)(2,1)}, u32[]{:S(2)}) copy-start(bf16[27,64,32]{1,2,0:T(8,128)(2,1)} %param.5) | copy-start | bytes 331780
  2.5 0.9 %copy-start.2 = (bf16[128,2,4,64]{0,3,2,1:T(8,128)(2,1)S(1)}, bf16[128,2,4,64]{0,3,2,1:T(8,128)(2,1)}, u32[]{:S(2)}) copy-start(bf16[128,2,4,64]{0,3,2,1:T(8,128)(2,1)} %param.7) | copy-start | bytes 393220
  3.4 0.8 %copy-start.3 = (bf16[27,8,64]{2,1,0:T(8,128)(2,1)S(1)}, bf16[27,8,64]{2,1,0:T(8,128)(2,1)}, u32[]{:S(2)}) copy-start(bf16[27,8,64]{2,1,0:T(8,128)(2,1)} %f4_hbm.1) | copy-start | bytes 82948

commit v4 on v3

--- a/solution.py
+++ b/solution.py
@@ -255,13 +255,13 @@
         for j in range(8):
             stack_row(1 + i, 1 + j)
 
+    fetches[3].wait()
+    stage("dilate", dilate)
+    halo_start(*halo_c)
     fetches[2].wait()
     stage("rows_f3", rows_f3)
-    fetches[3].wait()
-    stage("dilate", dilate)
     stage("stack_x", lambda: each(0, 4, stack_x))
     halo_wait(*halo_x)
-    halo_start(*halo_c)
 
     def stack_rim():
         for j in range(10):
@@ -538,9 +538,9 @@
     gv, g3, g4 = pl.pallas_call(
         kernel,
         out_shape=(
-            jax.ShapeDtypeStruct((32, 4, 8, 128), BF16),
-            jax.ShapeDtypeStruct((27, 32, 64), F32),
-            jax.ShapeDtypeStruct((27, 8, 64), F32),
+            pltpu.VMEM((32, 4, 8, 128), BF16),
+            pltpu.VMEM((27, 32, 64), F32),
+            pltpu.VMEM((27, 8, 64), F32),
         ),
         in_specs=[hbm] * 4,
         out_specs=(vmem,) * 3,
@@ -593,7 +593,7 @@
             dma((16,)),
         ],
         compiler_params=pltpu.CompilerParams(
-            collective_id=0, has_side_effects=True, vmem_limit_bytes=40 * 1024 * 1024
+            collective_id=0, has_side_effects=True, vmem_limit_bytes=58000 * 1024
         ),
     )(
         volume,

time: 56.9 us -> 51.1 us (0.90)
  local copies, waits for them, and re-layouts: 5.71 us -> 2.11 us
  Pallas kernels: 50.3 us -> 48.2 us
    unnamed x11 -> x3, local copies, waits for them, and re-layouts: 5.71 us -> 2.11 us
    pallas_call x1, Pallas kernels: 50.3 us -> 48.2 us  [shards(): pl.pallas_call(kernel, out_shape=(pltpu.VMEM((32, 4, 8, 128), BF16), pltp...]
where the time goes in v4:
time: 51.1 us; the launch traced here: 50.9 us
  Pallas kernels  48.2 us (94%)
  local copies, waits for them, and re-layouts  2.11 us (4%)
  between operations  0.64 us (1%)
    pallas_call x1, Pallas kernels, shards(): pl.pallas_call(kernel, out_shape=(pltpu.VMEM((32, 4, 8, 128), BF16), pltp...  48.2 us
    unnamed x3, local copies, waits for them, and re-layouts  2.11 us

profile of v4, /device:TPU:1, one launch (start us, length us, event | category | flops | bytes accessed | tf_op | source)
XLA Modules:
  0.0 50.9 jit_solution(15175291532579360798)
XLA Ops:
  0.6 48.2 %shard_map.67 = (bf16[32,4,8,128]{3,2,1,0:T(8,128)(2,1)S(1)}, f32[27,32,64]{2,1,0:T(8,128)S(1)}, f32[27,8,64]{2,1,0:T(8,128)S(1)}) custom-call(bf16[32,4,8,128]{3,2,1,0:T(8,128)(2,1)} %x_hbm.1, bf16[27,32,64]{2,1,0:T(8,128)(2,1)} %bitcast.4, bf16[27,8,64]{2,1,0:T(8,128)(2,1)} %f4_hbm.1, bf16[2,4,64,128]{3,2,1,0:T(8,128)(2,1)} %bitcast.5), custom_call_target="tpu_custom_call" | custom-call | tf_op jit(solution)/shard_map/pallas_call | solution.py:538
  48.8 0.7 %copy.10 = bf16[32,4,8,128]{3,2,1,0:T(8,128)(2,1)} copy(bf16[32,4,8,128]{3,2,1,0:T(8,128)(2,1)S(1)} %get-tuple-element.9) | data formatting | bytes 524288
  49.5 0.8 %copy.11 = f32[27,64,32]{1,2,0:T(8,128)} copy(f32[27,64,32]{1,2,0:T(8,128)S(1)} %bitcast.3) | data formatting | bytes 442368
  50.3 0.6 %copy.12 = f32[27,8,64]{2,1,0:T(8,128)} copy(f32[27,8,64]{2,1,0:T(8,128)S(1)} %get-tuple-element.11) | data formatting | bytes 110592

commit v5 on v4

--- a/solution.py
+++ b/solution.py
@@ -38,14 +38,15 @@
 
 def shifted(v, step):
     lane = lanes_iota(v.shape)
-    before = jnp.where(lane < step, 0.0, pltpu.roll(v, step, 1))
-    after = jnp.where(lane >= 128 - step, 0.0, pltpu.roll(v, 128 - step, 1))
+    zero = jnp.zeros((), v.dtype)
+    before = jnp.where(lane < step, zero, pltpu.roll(v, step, 1))
+    after = jnp.where(lane >= 128 - step, zero, pltpu.roll(v, 128 - step, 1))
     return before, after
 
 
 def stack_width(row, step):
-    before, after = shifted(row.astype(F32), step)
-    return jnp.concatenate([before.astype(BF16), row, after.astype(BF16)], axis=0)
+    before, after = shifted(row, step)
+    return jnp.concatenate([before, row, after], axis=0)
 
 
 def part(at, cells, width, far):
@@ -74,10 +75,10 @@
     x_hbm, f3_hbm, f4_hbm, cot_hbm,
     gv_out, g3_out, g4_out,
     x_in, f3, f4_in, cot, f4, a3, a6,
-    xb, xx, slope3, ck, pk, pq, dq, dv, d3, dd3, bank, a4, a5,
-    f4acc, r4, q4, t4, q4b,
+    xb, xx, slope3, ck, pk, pq, dq, dv, d3, dd3, rim, near, gown, bank, a4, a5,
+    f4acc, r4, q40, r4b, q4, t4, q4b,
     f3acc, r3, q3, t3, q3b, v3,
-    in_sem, halo_s, halo_r, ag_s, ag_r, s4_s, s4_r, b4_s, b4_r, s3_s, s3_r, b3_s, b3_r, c3_s, c3_r,
+    in_sem, halo_s, halo_r, s40_s, s40_r, ag_s, ag_r, s4_s, s4_r, b4_s, b4_r, s3_s, s3_r, b3_s, b3_r, c3_s, c3_r,
 ):
     d = lax.axis_index("depth")
     h = lax.axis_index("height")
@@ -137,10 +138,14 @@
     stage("rows_f4", rows_f4)
     pl.semaphore_wait(barrier, 8 + NH - 1 + ND - 3)
 
-    def halo_copy(which, n, buf, cells_d, cells_h, width):
+    def halo_copy(which, n, buf, cells_d, cells_h, width, beyond=None):
         dd, hh = DIRECTIONS[n]
+        if beyond is None:
+            src = buf.at[part(dd, cells_d, width, False), part(hh, cells_h, width, False)]
+        else:
+            src = beyond.at[part(-dd, cells_d, width, True), part(-hh, cells_h, width, True)]
         return pltpu.make_async_remote_copy(
-            src_ref=buf.at[part(dd, cells_d, width, False), part(hh, cells_h, width, False)],
+            src_ref=src,
             dst_ref=buf.at[part(dd, cells_d, width, True), part(hh, cells_h, width, True)],
             send_sem=halo_s.at[which, n],
             recv_sem=halo_r.at[which, n],
@@ -157,7 +162,7 @@
             halo_copy(which[0], n, *which[1:]).wait_send()
         for n in range(8):
             halo_copy(which[0], n, *which[1:]).wait_recv()
-        _, buf, cells_d, cells_h, width = which
+        _, buf, cells_d, cells_h, width = which[:5]
         channels = buf.shape[2]
         across = (width, cells_h + 2 * width, channels, 128)
         along = (cells_d + 2 * width, width, channels, 128)
@@ -222,7 +227,7 @@
     halo_x = (0, xb, 4, 8, 1)
     halo_p = (1, pk, 2, 4, 2)
     halo_c = (2, ck, 2, 4, 1)
-    halo_d3 = (3, d3, 4, 8, 1)
+    halo_g = (3, near, 4, 8, 1, rim)
     halo_start(*halo_x)
     each(1, NH, lambda k: gather_send(f4, bank, ag_s, ag_r, k).start())
     bank[h] = f4[...]
@@ -318,9 +323,7 @@
 
     def stack_p(i):
         for j in range(8):
-            both = two_rows(pk[i, j].astype(F32), pk[i + 2, j].astype(F32))
-            before, after = shifted(both, 2)
-            pq[i, j] = jnp.concatenate([before, both, after], axis=0).astype(BF16)
+            pq[i, j] = stack_width(two_rows(pk[i, j], pk[i + 2, j]), 2)
 
     stage("stack_p", lambda: each(0, 4, stack_p))
 
@@ -338,18 +341,18 @@
             _, slope = gelu_parts(act)
             for s in range(2):
                 col = 2 * j + s
-                both = two_rows(ck[i, col].astype(F32), ck[i + 2, col].astype(F32))
+                both = two_rows(ck[i, col], ck[i + 2, col]).astype(F32)
                 dq[i, col] = (both * slope[:, 128 * s : 128 * s + 128]).astype(BF16)
 
     stage("forward4", lambda: each(0, 2, forward4))
 
     def pair_rows():
         for j in range(6):
-            one, two = dq[0, j].astype(F32), dq[1, j].astype(F32)
+            one, two = dq[0, j], dq[1, j]
             even = lanes_iota(one.shape) % 2 == 0
-            dv[0, j] = interleave_odd(one, two).astype(BF16)
-            dv[1, j] = jnp.where(even, two, one).astype(BF16)
-            dv[2, j] = interleave(one, two).astype(BF16)
+            dv[0, j] = interleave_odd(one, two)
+            dv[1, j] = jnp.where(even, two, one)
+            dv[2, j] = interleave(one, two)
 
     stage("pair_rows", pair_rows)
 
@@ -373,14 +376,16 @@
                 for di in range(2):
                     for dj in range(2):
                         row, col = 2 * i + di, 2 * (2 * j + s) + dj
-                        delta = spread[i] * slope3[row, col]
+                        delta = (spread[i] * slope3[row, col]).astype(BF16)
                         before, after = shifted(delta, 1)
-                        stack = jnp.concatenate([after, delta, before], axis=0).astype(BF16)
-                        dd3[row, col] = stack
-                        d3[1 + row, 1 + col] = stack[64:128]
+                        dd3[row, col] = jnp.concatenate([after, delta, before], axis=0)
+                        d3[1 + row, 1 + col] = delta
 
     stage("back4", lambda: each(0, 2, back4))
-    halo_start(*halo_d3)
+    d3[0] = jnp.zeros((10, 64, 128), BF16)
+    d3[5] = jnp.zeros((10, 64, 128), BF16)
+    d3[:, 0] = jnp.zeros((6, 64, 128), BF16)
+    d3[:, 9] = jnp.zeros((6, 64, 128), BF16)
 
     f3acc[...] = jnp.zeros(f3acc.shape, F32)
 
@@ -422,11 +427,11 @@
         even = lanes_iota((128, 128)) % 2 == 0
         left = jnp.concatenate(
             [
-                jnp.where(even if i == 0 else ~even, dq[1 - i, 1 + j].astype(F32), 0.0)
+                jnp.where(even if i == 0 else ~even, dq[1 - i, 1 + j], jnp.zeros((), BF16))
                 for i, j in cells4
             ],
             axis=1,
-        ).astype(BF16)
+        )
         for g in range(5):
             taps = [ab for ab in (2 * g, 2 * g + 1) if ab < 9]
             right = jnp.concatenate(
@@ -449,30 +454,96 @@
 
     def pack4(s):
         rows = pl.ds(pl.multiple_of(8 * s, 8), 8)
-        r4[s] = jnp.concatenate([f4acc[rows, :896], f4acc[rows, 896:]], axis=0).astype(BF16)
+        r4[lax.rem(s, 2), s // 2] = jnp.concatenate(
+            [f4acc[rows, :896], f4acc[rows, 896:]], axis=0
+        ).astype(BF16)
 
     stage("pack4", lambda: each(0, NH, pack4))
-    each(1, NH, lambda k: scatter_h(r4, q4, s4_s, s4_r, k).start())
+    core = lax.rem(h, 2)
+    pair = h // 2
+
+    def swap4():
+        return pltpu.make_async_remote_copy(
+            src_ref=r4.at[1 - core],
+            dst_ref=q40,
+            send_sem=s40_s,
+            recv_sem=s40_r,
+            device_id=(d, h + 1 - 2 * core),
+            device_id_type=MESH,
+        )
+
+    def scatter4(k):
+        other = lax.rem(pair + k, NH // 2)
+        return pltpu.make_async_remote_copy(
+            src_ref=r4b.at[other],
+            dst_ref=q4.at[k],
+            send_sem=s4_s.at[k],
+            recv_sem=s4_r.at[k],
+            device_id=partner(2 * other + core),
+            device_id_type=MESH,
+        )
+
+    swap4().start()
+
+    def gather_width(y, s):
+        ys = y[:, 128 * s : 128 * s + 128]
+        _, from_after = shifted(ys[:32], 1)
+        from_before, _ = shifted(ys[64:], 1)
+        return ys[32:64] + from_after + from_before
+
+    def back_rim():
+        for j in range(5):
+            for a, row in ((0, 0), (2, 5)):
+                source = 1 if row == 0 else 4
+                cols = [
+                    jnp.concatenate(
+                        [
+                            d3[source, 2 * j + s + 1 - b]
+                            if 0 <= 2 * j + s + 1 - b <= 9
+                            else jnp.zeros((64, 128), BF16)
+                            for b in range(3)
+                        ],
+                        axis=0,
+                    )
+                    for s in range(2)
+                ]
+                y = jnp.dot(
+                    a6[:, 192 * a : 192 * a + 192],
+                    jnp.concatenate(cols, axis=1),
+                    preferred_element_type=F32,
+                )
+                for s in range(2):
+                    rim[row, 2 * j + s] = gather_width(y, s).astype(BF16)
+        for b, col, source in ((0, 0, 1), (2, 9, 8)):
+            weights = jnp.concatenate(
+                [a6[:, 192 * a + 64 * b : 192 * a + 64 * b + 64] for a in range(3)], axis=1
+            )
+            for i in range(2):
+                cols = [
+                    jnp.concatenate([d3[2 * i + s + 2 - a, source] for a in range(3)], axis=0)
+                    for s in range(2)
+                ]
+                y = jnp.dot(weights, jnp.concatenate(cols, axis=1), preferred_element_type=F32)
+                for s in range(2):
+                    rim[1 + 2 * i + s, col] = gather_width(y, s).astype(BF16)
+
+    stage("back_rim", back_rim)
+    halo_start(*halo_g)
 
     def wait_both(copy):
         copy.wait_send()
         copy.wait_recv()
 
-    each(1, NH, lambda k: wait_both(scatter_h(r3, q3, s3_s, s3_r, k)))
-
-    def sum3():
-        total3 = r3[h].astype(F32)
-        for k in range(1, NH):
-            total3 = total3 + q3[k].astype(F32)
-        t3[...] = total3
-
-    stage("sum3", sum3)
-    each(1, ND, lambda k: share_d(t3, q3b, b3_s, b3_r, k).start())
-
-    halo_wait(*halo_d3)
+    wait_both(swap4())
+
+    def add4():
+        for m in range(8):
+            r4b[m] = (r4[core, m].astype(F32) + q40[m].astype(F32)).astype(BF16)
+
+    stage("add4", add4)
+    each(1, NH // 2, lambda k: scatter4(k).start())
 
     def back3(i):
-        done = []
         for j in range(4):
             cols = [
                 jnp.concatenate(
@@ -482,19 +553,45 @@
             ]
             y = jnp.dot(a6[...], jnp.concatenate(cols, axis=1), preferred_element_type=F32)
             for s in range(2):
-                ys = y[:, 128 * s : 128 * s + 128]
-                _, from_after = shifted(ys[:32], 1)
-                from_before, _ = shifted(ys[64:], 1)
-                done.append(ys[32:64] + from_after + from_before)
-        gv_out[:, i] = jnp.transpose(jnp.stack(done, axis=0), (1, 0, 2)).astype(BF16)
-
-    stage("back3", lambda: each(0, 4, back3))
-
-    each(1, NH, lambda k: wait_both(scatter_h(r4, q4, s4_s, s4_r, k)))
+                gown[i, 2 * j + s] = gather_width(y, s)
+
+    stage("back3a", lambda: each(0, 2, back3))
+
+    each(1, NH, lambda k: wait_both(scatter_h(r3, q3, s3_s, s3_r, k)))
+
+    def sum3():
+        total3 = r3[h].astype(F32)
+        for k in range(1, NH):
+            total3 = total3 + q3[k].astype(F32)
+        t3[...] = total3
+
+    stage("sum3", sum3)
+    each(1, ND, lambda k: share_d(t3, q3b, b3_s, b3_r, k).start())
+    stage("back3b", lambda: each(2, 4, back3))
+
+    halo_wait(*halo_g)
+
+    def finish_gv():
+        for i in range(4):
+            done = []
+            for j in range(8):
+                total = gown[i, j]
+                if i in (0, 3):
+                    total = total + near[0 if i == 0 else 5, 1 + j].astype(F32)
+                if j in (0, 7):
+                    total = total + near[1 + i, 0 if j == 0 else 9].astype(F32)
+                if i in (0, 3) and j in (0, 7):
+                    total = total + near[0 if i == 0 else 5, 0 if j == 0 else 9].astype(F32)
+                done.append(total)
+            gv_out[:, i] = jnp.transpose(jnp.stack(done, axis=0), (1, 0, 2)).astype(BF16)
+
+    stage("finish_gv", finish_gv)
+
+    each(1, NH // 2, lambda k: wait_both(scatter4(k)))
 
     def sum4():
-        total4 = r4[h].astype(F32)
-        for k in range(1, NH):
+        total4 = r4b[pair].astype(F32)
+        for k in range(1, NH // 2):
             total4 = total4 + q4[k].astype(F32)
         t4[...] = total4.astype(BF16)
 
@@ -562,12 +659,17 @@
             pltpu.VMEM((3, 6, 128, 128), BF16),
             pltpu.VMEM((6, 10, 64, 128), BF16),
             pltpu.VMEM((4, 8, 192, 128), BF16),
+            pltpu.VMEM((6, 10, 32, 128), BF16),
+            pltpu.VMEM((6, 10, 32, 128), BF16),
+            pltpu.VMEM((4, 8, 32, 128), F32),
             pltpu.VMEM((16, 16, 896), BF16),
             pltpu.VMEM((128, 1792), BF16),
             pltpu.VMEM((192, 1152), BF16),
             pltpu.VMEM((128, 1792), F32),
-            pltpu.VMEM((16, 16, 896), BF16),
-            pltpu.VMEM((16, 16, 896), BF16),
+            pltpu.VMEM((2, 8, 16, 896), BF16),
+            pltpu.VMEM((8, 16, 896), BF16),
+            pltpu.VMEM((8, 16, 896), BF16),
+            pltpu.VMEM((8, 16, 896), BF16),
             pltpu.VMEM((16, 896), BF16),
             pltpu.VMEM((8, 16, 896), BF16),
             pltpu.VMEM((288, 192), F32),
@@ -579,6 +681,8 @@
             dma((4,)),
             dma((4, 8)),
             dma((4, 8)),
+            dma,
+            dma,
             dma((16,)),
             dma((16,)),
             dma((16,)),

time: 51.1 us -> 50 us (0.978)
  Pallas kernels: 48.2 us -> 47.1 us
    pallas_call x1, Pallas kernels: 48.2 us -> 47.1 us  [shards(): pl.pallas_call(kernel, out_shape=(pltpu.VMEM((32, 4, 8, 128), BF16), pltp...]
where the time goes in v5:
time: 50 us; the launch traced here: 49.9 us
  Pallas kernels  47.1 us (94%)
  local copies, waits for them, and re-layouts  2.11 us (4%)
  between operations  0.64 us (1%)
    pallas_call x1, Pallas kernels, shards(): pl.pallas_call(kernel, out_shape=(pltpu.VMEM((32, 4, 8, 128), BF16), pltp...  47.1 us
    unnamed x3, local copies, waits for them, and re-layouts  2.11 us

profile of v5, /device:TPU:1, one launch (start us, length us, event | category | flops | bytes accessed | tf_op | source)
XLA Modules:
  0.0 49.9 jit_solution(16357159991446987521)
XLA Ops:
  0.6 47.1 %shard_map.67 = (bf16[32,4,8,128]{3,2,1,0:T(8,128)(2,1)S(1)}, f32[27,32,64]{2,1,0:T(8,128)S(1)}, f32[27,8,64]{2,1,0:T(8,128)S(1)}) custom-call(bf16[32,4,8,128]{3,2,1,0:T(8,128)(2,1)} %x_hbm.1, bf16[27,32,64]{2,1,0:T(8,128)(2,1)} %bitcast.4, bf16[27,8,64]{2,1,0:T(8,128)(2,1)} %f4_hbm.1, bf16[2,4,64,128]{3,2,1,0:T(8,128)(2,1)} %bitcast.5), custom_call_target="tpu_custom_call" | custom-call | tf_op jit(solution)/shard_map/pallas_call | solution.py:635
  47.8 0.7 %copy.10 = bf16[32,4,8,128]{3,2,1,0:T(8,128)(2,1)} copy(bf16[32,4,8,128]{3,2,1,0:T(8,128)(2,1)S(1)} %get-tuple-element.9) | data formatting | bytes 524288
  48.5 0.8 %copy.11 = f32[27,64,32]{1,2,0:T(8,128)} copy(f32[27,64,32]{1,2,0:T(8,128)S(1)} %bitcast.3) | data formatting | bytes 442368
  49.2 0.6 %copy.12 = f32[27,8,64]{2,1,0:T(8,128)} copy(f32[27,8,64]{2,1,0:T(8,128)S(1)} %get-tuple-element.11) | data formatting | bytes 110592

commit v6 on v5

--- a/solution.py
+++ b/solution.py
@@ -419,7 +419,8 @@
             r3[c] = flat[32 * c : 32 * c + 32]
 
     stage("pack3", pack3)
-    each(1, NH, lambda k: scatter_h(r3, q3, s3_s, s3_r, k).start())
+    for k in range(1, NH):
+        scatter_h(r3, q3, s3_s, s3_r, k).start()
 
     cells4 = [(i, j) for i in range(2) for j in range(4)]
 
@@ -557,16 +558,18 @@
 
     stage("back3a", lambda: each(0, 2, back3))
 
-    each(1, NH, lambda k: wait_both(scatter_h(r3, q3, s3_s, s3_r, k)))
+    for k in range(1, NH):
+        wait_both(scatter_h(r3, q3, s3_s, s3_r, k))
 
     def sum3():
         total3 = r3[h].astype(F32)
         for k in range(1, NH):
             total3 = total3 + q3[k].astype(F32)
-        t3[...] = total3
+        t3[...] = total3.astype(BF16)
 
     stage("sum3", sum3)
-    each(1, ND, lambda k: share_d(t3, q3b, b3_s, b3_r, k).start())
+    for k in range(1, ND):
+        share_d(t3, q3b, b3_s, b3_r, k).start()
     stage("back3b", lambda: each(2, 4, back3))
 
     halo_wait(*halo_g)
@@ -598,12 +601,14 @@
     stage("sum4", sum4)
     each(1, ND, lambda k: share_d(t4, q4b, b4_s, b4_r, k).start())
 
-    each(1, ND, lambda k: wait_both(share_d(t3, q3b, b3_s, b3_r, k)))
-    whole3 = t3[...]
     for k in range(1, ND):
-        whole3 = whole3 + q3b[k]
+        wait_both(share_d(t3, q3b, b3_s, b3_r, k))
+    whole3 = t3[...].astype(F32)
+    for k in range(1, ND):
+        whole3 = whole3 + q3b[k].astype(F32)
     v3[h] = (whole3 * (1.0 / math.sqrt(32 * 128 * 128))).astype(BF16)
-    each(1, NH, lambda k: gather_send(v3.at[h], v3, c3_s, c3_r, k).start())
+    for k in range(1, NH):
+        gather_send(v3.at[h], v3, c3_s, c3_r, k).start()
 
     each(1, ND, lambda k: wait_both(share_d(t4, q4b, b4_s, b4_r, k)))
     whole4 = t4[...].astype(F32)
@@ -618,7 +623,8 @@
         gather_send(v3.at[h], v3, c3_s, c3_r, k).wait_send()
         gather_recv(v3.at[h], v3, c3_s, c3_r, k).wait_recv()
 
-    each(1, NH, wait_c3)
+    for k in range(1, NH):
+        wait_c3(k)
     flat3 = jnp.concatenate([v3[c].astype(F32) for c in range(14)], axis=0)
     last3 = jnp.concatenate([flat3[288:432, :64], flat3[288:432, 64:]], axis=0)
     for ab in range(9):
@@ -626,6 +632,17 @@
         g3_out[3 * ab] = flat3[rows, :64]
         g3_out[3 * ab + 1] = flat3[rows, 64:]
         g3_out[3 * ab + 2] = last3[rows]
+
+
+def writer(gv, g3, g4, gv_hbm, g3_hbm, g4_hbm, sems):
+    copies = [
+        pltpu.make_async_copy(src, dst, sems.at[n])
+        for n, (src, dst) in enumerate([(gv, gv_hbm), (g3, g3_hbm), (g4, g4_hbm)])
+    ]
+    for copy in copies:
+        copy.start()
+    for copy in copies:
+        copy.wait()
 
 
 def shards(volume, filters_three, filters_four, cotangent):
@@ -675,8 +692,8 @@
             pltpu.VMEM((288, 192), F32),
             pltpu.VMEM((16, 32, 128), BF16),
             pltpu.VMEM((16, 32, 128), BF16),
-            pltpu.VMEM((32, 128), F32),
-            pltpu.VMEM((8, 32, 128), F32),
+            pltpu.VMEM((32, 128), BF16),
+            pltpu.VMEM((8, 32, 128), BF16),
             pltpu.VMEM((16, 32, 128), BF16),
             dma((4,)),
             dma((4, 8)),
@@ -705,6 +722,18 @@
         filters_four,
         jnp.transpose(cotangent, (1, 2, 3, 0)),
     )
+    gv, g3, g4 = pl.pallas_call(
+        writer,
+        out_shape=(
+            pltpu.HBM((32, 4, 8, 128), BF16),
+            pltpu.HBM((27, 32, 64), F32),
+            pltpu.HBM((27, 8, 64), F32),
+        ),
+        in_specs=[hbm] * 3,
+        out_specs=(hbm,) * 3,
+        scratch_shapes=[dma((3,))],
+        compiler_params=pltpu.CompilerParams(vmem_limit_bytes=1024 * 1024),
+    )(gv, g3, g4)
     return (gv, jnp.transpose(g3, (0, 2, 1)), g4)
 
 

time: 50 us -> 48.1 us (0.962)
  local copies, waits for them, and re-layouts: 2.11 us -> 0 us
    unnamed x3 -> x0, local copies, waits for them, and re-layouts: 2.11 us -> none
    pallas_call x0 -> x1, Pallas kernels: none -> 0.91 us  [shards(): pl.pallas_call(writer, out_shape=(pltpu.HBM((32, 4, 8, 128), BF16), pltpu...]
    pallas_call x1, Pallas kernels: 47.1 us -> 46.5 us  [shards(): pl.pallas_call(kernel, out_shape=(pltpu.VMEM((32, 4, 8, 128), BF16), pltp...]
where the time goes in v6:
time: 48.1 us; the launch traced here: 48 us
  Pallas kernels  47.4 us (99%)
  between operations  0.64 us (1%)
    pallas_call x1, Pallas kernels, shards(): pl.pallas_call(kernel, out_shape=(pltpu.VMEM((32, 4, 8, 128), BF16), pltp...  46.5 us

profile of v6, /device:TPU:1, one launch (start us, length us, event | category | flops | bytes accessed | tf_op | source)
XLA Modules:
  0.0 48.0 jit_solution(15300194857416542194)
XLA Ops:
  0.6 46.5 %shard_map.67 = (bf16[32,4,8,128]{3,2,1,0:T(8,128)(2,1)S(1)}, f32[27,32,64]{2,1,0:T(8,128)S(1)}, f32[27,8,64]{2,1,0:T(8,128)S(1)}) custom-call(bf16[32,4,8,128]{3,2,1,0:T(8,128)(2,1)} %x_hbm.1, bf16[27,32,64]{2,1,0:T(8,128)(2,1)} %bitcast.3, bf16[27,8,64]{2,1,0:T(8,128)(2,1)} %f4_hbm.1, bf16[2,4,64,128]{3,2,1,0:T(8,128)(2,1)} %bitcast.4), custom_call_target="tpu_custom_call" | custom-call | tf_op jit(solution)/shard_map/pallas_call | solution.py:652
  47.1 0.9 %shard_map.68 = (bf16[32,4,8,128]{3,2,1,0:T(8,128)(2,1)}, f32[27,32,64]{2,1,0:T(8,128)}, f32[27,8,64]{2,1,0:T(8,128)}) custom-call(bf16[32,4,8,128]{3,2,1,0:T(8,128)(2,1)S(1)} %get-tuple-element.9.gv, f32[27,32,64]{2,1,0:T(8,128)S(1)} %get-tuple-element.10.g3, f32[27,8,64]{2,1,0:T(8,128)S(1)} %get-tuple-element.11.g4), custom_call_target="tpu_custom_call" | custom-call | tf_op jit(solution)/shard_map/pallas_call | solution.py:725

commit v7 on v6

--- a/solution.py
+++ b/solution.py
@@ -266,6 +266,10 @@
     fetches[2].wait()
     stage("rows_f3", rows_f3)
     stage("stack_x", lambda: each(0, 4, stack_x))
+    d3[0] = jnp.zeros((10, 64, 128), BF16)
+    d3[5] = jnp.zeros((10, 64, 128), BF16)
+    d3[:, 0] = jnp.zeros((6, 64, 128), BF16)
+    d3[:, 9] = jnp.zeros((6, 64, 128), BF16)
     halo_wait(*halo_x)
 
     def stack_rim():
@@ -298,7 +302,7 @@
             total = (total + pltpu.roll(total, 127, 1)) * 0.125
             pk[2 + i, 2 + j] = interleave(total[:32], total[32:]).astype(BF16)
 
-    stage("forward3", lambda: each(0, 2, forward3))
+    stage("forward3", lambda: [forward3(n) for n in range(0, 2)])
     halo_start(*halo_p)
 
     def wait_gather(k):
@@ -325,7 +329,7 @@
         for j in range(8):
             pq[i, j] = stack_width(two_rows(pk[i, j], pk[i + 2, j]), 2)
 
-    stage("stack_p", lambda: each(0, 4, stack_p))
+    stage("stack_p", lambda: [stack_p(n) for n in range(0, 4)])
 
     def forward4(i):
         for j in range(3):
@@ -344,7 +348,7 @@
                 both = two_rows(ck[i, col], ck[i + 2, col]).astype(F32)
                 dq[i, col] = (both * slope[:, 128 * s : 128 * s + 128]).astype(BF16)
 
-    stage("forward4", lambda: each(0, 2, forward4))
+    stage("forward4", lambda: [forward4(n) for n in range(0, 2)])
 
     def pair_rows():
         for j in range(6):
@@ -381,11 +385,7 @@
                         dd3[row, col] = jnp.concatenate([after, delta, before], axis=0)
                         d3[1 + row, 1 + col] = delta
 
-    stage("back4", lambda: each(0, 2, back4))
-    d3[0] = jnp.zeros((10, 64, 128), BF16)
-    d3[5] = jnp.zeros((10, 64, 128), BF16)
-    d3[:, 0] = jnp.zeros((6, 64, 128), BF16)
-    d3[:, 9] = jnp.zeros((6, 64, 128), BF16)
+    stage("back4", lambda: [back4(n) for n in range(0, 2)])
 
     f3acc[...] = jnp.zeros(f3acc.shape, F32)
 
@@ -403,7 +403,7 @@
             left, right, (((1,), (1,)), ((), ())), preferred_element_type=F32
         )
 
-    stage("weight3", lambda: each(0, 4, weight3))
+    stage("weight3", lambda: [weight3(n) for n in range(0, 4)])
 
     def pack3():
         last = f3acc[:, 128:]
@@ -556,7 +556,7 @@
             for s in range(2):
                 gown[i, 2 * j + s] = gather_width(y, s)
 
-    stage("back3a", lambda: each(0, 2, back3))
+    stage("back3a", lambda: [back3(n) for n in range(0, 2)])
 
     for k in range(1, NH):
         wait_both(scatter_h(r3, q3, s3_s, s3_r, k))
@@ -570,7 +570,27 @@
     stage("sum3", sum3)
     for k in range(1, ND):
         share_d(t3, q3b, b3_s, b3_r, k).start()
-    stage("back3b", lambda: each(2, 4, back3))
+    stage("back3b", lambda: [back3(n) for n in range(2, 4)])
+
+    each(1, NH // 2, lambda k: wait_both(scatter4(k)))
+
+    def sum4():
+        total4 = r4b[pair].astype(F32)
+        for k in range(1, NH // 2):
+            total4 = total4 + q4[k].astype(F32)
+        t4[...] = total4.astype(BF16)
+
+    stage("sum4", sum4)
+    each(1, ND, lambda k: share_d(t4, q4b, b4_s, b4_r, k).start())
+
+    for k in range(1, ND):
+        wait_both(share_d(t3, q3b, b3_s, b3_r, k))
+    whole3 = t3[...].astype(F32)
+    for k in range(1, ND):
+        whole3 = whole3 + q3b[k].astype(F32)
+    v3[h] = (whole3 * (1.0 / math.sqrt(32 * 128 * 128))).astype(BF16)
+    for k in range(1, NH):
+        gather_send(v3.at[h], v3, c3_s, c3_r, k).start()
 
     halo_wait(*halo_g)
 
@@ -589,26 +609,6 @@
             gv_out[:, i] = jnp.transpose(jnp.stack(done, axis=0), (1, 0, 2)).astype(BF16)
 
     stage("finish_gv", finish_gv)
-
-    each(1, NH // 2, lambda k: wait_both(scatter4(k)))
-
-    def sum4():
-        total4 = r4b[pair].astype(F32)
-        for k in range(1, NH // 2):
-            total4 = total4 + q4[k].astype(F32)
-        t4[...] = total4.astype(BF16)
-
-    stage("sum4", sum4)
-    each(1, ND, lambda k: share_d(t4, q4b, b4_s, b4_r, k).start())
-
-    for k in range(1, ND):
-        wait_both(share_d(t3, q3b, b3_s, b3_r, k))
-    whole3 = t3[...].astype(F32)
-    for k in range(1, ND):
-        whole3 = whole3 + q3b[k].astype(F32)
-    v3[h] = (whole3 * (1.0 / math.sqrt(32 * 128 * 128))).astype(BF16)
-    for k in range(1, NH):
-        gather_send(v3.at[h], v3, c3_s, c3_r, k).start()
 
     each(1, ND, lambda k: wait_both(share_d(t4, q4b, b4_s, b4_r, k)))
     whole4 = t4[...].astype(F32)

time: 48.1 us -> 46.3 us (0.963)
  Pallas kernels: 47.4 us -> 45.5 us
    pallas_call x1, Pallas kernels: 46.5 us -> 44.6 us  [shards(): pl.pallas_call(kernel, out_shape=(pltpu.VMEM((32, 4, 8, 128), BF16), pltp...]
where the time goes in v7:
time: 46.3 us; the launch traced here: 46.1 us
  Pallas kernels  45.5 us (98%)
  between operations  0.64 us (1%)
    pallas_call x1, Pallas kernels, shards(): pl.pallas_call(kernel, out_shape=(pltpu.VMEM((32, 4, 8, 128), BF16), pltp...  44.6 us

profile of v7, /device:TPU:1, one launch (start us, length us, event | category | flops | bytes accessed | tf_op | source)
XLA Modules:
  0.0 46.1 jit_solution(122945547362969559)
XLA Ops:
  0.6 44.6 %shard_map.67 = (bf16[32,4,8,128]{3,2,1,0:T(8,128)(2,1)S(1)}, f32[27,32,64]{2,1,0:T(8,128)S(1)}, f32[27,8,64]{2,1,0:T(8,128)S(1)}) custom-call(bf16[32,4,8,128]{3,2,1,0:T(8,128)(2,1)} %x_hbm.1, bf16[27,32,64]{2,1,0:T(8,128)(2,1)} %bitcast.3, bf16[27,8,64]{2,1,0:T(8,128)(2,1)} %f4_hbm.1, bf16[2,4,64,128]{3,2,1,0:T(8,128)(2,1)} %bitcast.4), custom_call_target="tpu_custom_call" | custom-call | tf_op jit(solution)/shard_map/pallas_call | solution.py:652
  45.2 0.9 %shard_map.68 = (bf16[32,4,8,128]{3,2,1,0:T(8,128)(2,1)}, f32[27,32,64]{2,1,0:T(8,128)}, f32[27,8,64]{2,1,0:T(8,128)}) custom-call(bf16[32,4,8,128]{3,2,1,0:T(8,128)(2,1)S(1)} %get-tuple-element.9.gv, f32[27,32,64]{2,1,0:T(8,128)S(1)} %get-tuple-element.10.g3, f32[27,8,64]{2,1,0:T(8,128)S(1)} %get-tuple-element.11.g4), custom_call_target="tpu_custom_call" | custom-call | tf_op jit(solution)/shard_map/pallas_call | solution.py:725

commit v8 on v7

--- a/solution.py
+++ b/solution.py
@@ -153,6 +153,17 @@
             device_id_type=MESH,
         )
 
+    def pooled_copy(row, n):
+        dd, hh = DIRECTIONS[n]
+        return pltpu.make_async_remote_copy(
+            src_ref=pk.at[pl.ds(2 + row, 1), part(hh, 4, 2, False)],
+            dst_ref=pk.at[pl.ds(2 - 2 * dd + row, 1), part(hh, 4, 2, True)],
+            send_sem=halo_s.at[1 + 3 * row, n],
+            recv_sem=halo_r.at[1 + 3 * row, n],
+            device_id=around(dd, hh),
+            device_id_type=MESH,
+        )
+
     def halo_start(*which):
         for n in range(8):
             halo_copy(which[0], n, *which[1:]).start()
@@ -162,7 +173,9 @@
             halo_copy(which[0], n, *which[1:]).wait_send()
         for n in range(8):
             halo_copy(which[0], n, *which[1:]).wait_recv()
-        _, buf, cells_d, cells_h, width = which[:5]
+        zero_outside(*which[1:5])
+
+    def zero_outside(buf, cells_d, cells_h, width):
         channels = buf.shape[2]
         across = (width, cells_h + 2 * width, channels, 128)
         along = (cells_d + 2 * width, width, channels, 128)
@@ -225,7 +238,6 @@
         )
 
     halo_x = (0, xb, 4, 8, 1)
-    halo_p = (1, pk, 2, 4, 2)
     halo_c = (2, ck, 2, 4, 1)
     halo_g = (3, near, 4, 8, 1, rim)
     halo_start(*halo_x)
@@ -302,8 +314,12 @@
             total = (total + pltpu.roll(total, 127, 1)) * 0.125
             pk[2 + i, 2 + j] = interleave(total[:32], total[32:]).astype(BF16)
 
-    stage("forward3", lambda: [forward3(n) for n in range(0, 2)])
-    halo_start(*halo_p)
+    def forward_and_send(i):
+        forward3(i)
+        for n in range(8):
+            pooled_copy(i, n).start()
+
+    stage("forward3", lambda: [forward_and_send(n) for n in range(0, 2)])
 
     def wait_gather(k):
         gather_send(f4, bank, ag_s, ag_r, k).wait_send()
@@ -323,7 +339,12 @@
 
     stage("arrange", arrange)
     halo_wait(*halo_c)
-    halo_wait(*halo_p)
+    for row in range(2):
+        for n in range(8):
+            pooled_copy(row, n).wait_send()
+        for n in range(8):
+            pooled_copy(row, n).wait_recv()
+    zero_outside(pk, 2, 4, 2)
 
     def stack_p(i):
         for j in range(8):
@@ -572,17 +593,6 @@
         share_d(t3, q3b, b3_s, b3_r, k).start()
     stage("back3b", lambda: [back3(n) for n in range(2, 4)])
 
-    each(1, NH // 2, lambda k: wait_both(scatter4(k)))
-
-    def sum4():
-        total4 = r4b[pair].astype(F32)
-        for k in range(1, NH // 2):
-            total4 = total4 + q4[k].astype(F32)
-        t4[...] = total4.astype(BF16)
-
-    stage("sum4", sum4)
-    each(1, ND, lambda k: share_d(t4, q4b, b4_s, b4_r, k).start())
-
     for k in range(1, ND):
         wait_both(share_d(t3, q3b, b3_s, b3_r, k))
     whole3 = t3[...].astype(F32)
@@ -591,6 +601,17 @@
     v3[h] = (whole3 * (1.0 / math.sqrt(32 * 128 * 128))).astype(BF16)
     for k in range(1, NH):
         gather_send(v3.at[h], v3, c3_s, c3_r, k).start()
+
+    each(1, NH // 2, lambda k: wait_both(scatter4(k)))
+
+    def sum4():
+        total4 = r4b[pair].astype(F32)
+        for k in range(1, NH // 2):
+            total4 = total4 + q4[k].astype(F32)
+        t4[...] = total4.astype(BF16)
+
+    stage("sum4", sum4)
+    each(1, ND, lambda k: share_d(t4, q4b, b4_s, b4_r, k).start())
 
     halo_wait(*halo_g)
 
@@ -696,8 +717,8 @@
             pltpu.VMEM((8, 32, 128), BF16),
             pltpu.VMEM((16, 32, 128), BF16),
             dma((4,)),
-            dma((4, 8)),
-            dma((4, 8)),
+            dma((5, 8)),
+            dma((5, 8)),
             dma,
             dma,
             dma((16,)),

time: 46.3 us -> 45.9 us (level)
  no operation moved by 1% of the time
where the time goes in v8:
time: 45.9 us; the launch traced here: 45.8 us
  Pallas kernels  45.1 us (98%)
  between operations  0.64 us (1%)
    pallas_call x1, Pallas kernels, shards(): pl.pallas_call(kernel, out_shape=(pltpu.VMEM((32, 4, 8, 128), BF16), pltp...  44.2 us

profile of v8, /device:TPU:1, one launch (start us, length us, event | category | flops | bytes accessed | tf_op | source)
XLA Modules:
  0.0 45.8 jit_solution(506607959799421212)
XLA Ops:
  0.6 44.2 %shard_map.67 = (bf16[32,4,8,128]{3,2,1,0:T(8,128)(2,1)S(1)}, f32[27,32,64]{2,1,0:T(8,128)S(1)}, f32[27,8,64]{2,1,0:T(8,128)S(1)}) custom-call(bf16[32,4,8,128]{3,2,1,0:T(8,128)(2,1)} %x_hbm.1, bf16[27,32,64]{2,1,0:T(8,128)(2,1)} %bitcast.3, bf16[27,8,64]{2,1,0:T(8,128)(2,1)} %f4_hbm.1, bf16[2,4,64,128]{3,2,1,0:T(8,128)(2,1)} %bitcast.4), custom_call_target="tpu_custom_call" | custom-call | tf_op jit(solution)/shard_map/pallas_call | solution.py:673
  44.9 0.9 %shard_map.68 = (bf16[32,4,8,128]{3,2,1,0:T(8,128)(2,1)}, f32[27,32,64]{2,1,0:T(8,128)}, f32[27,8,64]{2,1,0:T(8,128)}) custom-call(bf16[32,4,8,128]{3,2,1,0:T(8,128)(2,1)S(1)} %get-tuple-element.9.gv, f32[27,32,64]{2,1,0:T(8,128)S(1)} %get-tuple-element.10.g3, f32[27,8,64]{2,1,0:T(8,128)S(1)} %get-tuple-element.11.g4), custom_call_target="tpu_custom_call" | custom-call | tf_op jit(solution)/shard_map/pallas_call | solution.py:746

commit v9 on v8

--- a/solution.py
+++ b/solution.py
@@ -16,6 +16,7 @@
 
 ND = 8
 NH = 16
+FILLED = 14
 DIRECTIONS = [(dd, hh) for dd in (-1, 0, 1) for hh in (-1, 0, 1) if (dd, hh) != (0, 0)]
 
 
@@ -440,8 +441,13 @@
             r3[c] = flat[32 * c : 32 * c + 32]
 
     stage("pack3", pack3)
-    for k in range(1, NH):
-        scatter_h(r3, q3, s3_s, s3_r, k).start()
+    def scatter3(k):
+        @pl.when(lax.rem(h + k, NH) < FILLED)
+        def _():
+            scatter_h(r3, q3, s3_s, s3_r, k).start()
+
+    for k in (8, 9, 7, 10, 6, 11, 5, 12, 4, 13, 3, 14, 2, 15, 1):
+        scatter3(k)
 
     cells4 = [(i, j) for i in range(2) for j in range(4)]
 
@@ -579,14 +585,24 @@
 
     stage("back3a", lambda: [back3(n) for n in range(0, 2)])
 
+    def wait_3(k):
+        @pl.when(lax.rem(h + k, NH) < FILLED)
+        def _():
+            scatter_h(r3, q3, s3_s, s3_r, k).wait_send()
+
     for k in range(1, NH):
-        wait_both(scatter_h(r3, q3, s3_s, s3_r, k))
+        wait_3(k)
+
+    @pl.when(h < FILLED)
+    def _():
+        for k in range(1, NH):
+            scatter_h(r3, q3, s3_s, s3_r, k).wait_recv()
 
     def sum3():
         total3 = r3[h].astype(F32)
         for k in range(1, NH):
             total3 = total3 + q3[k].astype(F32)
-        t3[...] = total3.astype(BF16)
+        t3[...] = jnp.where(h < FILLED, total3, 0.0).astype(BF16)
 
     stage("sum3", sum3)
     for k in range(1, ND):
@@ -599,8 +615,10 @@
     for k in range(1, ND):
         whole3 = whole3 + q3b[k].astype(F32)
     v3[h] = (whole3 * (1.0 / math.sqrt(32 * 128 * 128))).astype(BF16)
-    for k in range(1, NH):
-        gather_send(v3.at[h], v3, c3_s, c3_r, k).start()
+    @pl.when(h < FILLED)
+    def _():
+        for k in (8, 9, 7, 10, 6, 11, 5, 12, 4, 13, 3, 14, 2, 15, 1):
+            gather_send(v3.at[h], v3, c3_s, c3_r, k).start()
 
     each(1, NH // 2, lambda k: wait_both(scatter4(k)))
 
@@ -641,11 +659,18 @@
         g4_out[t] = whole4[rows : rows + 8, lane : lane + 64]
 
     def wait_c3(k):
-        gather_send(v3.at[h], v3, c3_s, c3_r, k).wait_send()
-        gather_recv(v3.at[h], v3, c3_s, c3_r, k).wait_recv()
+        @pl.when(lax.rem(h - k + NH, NH) < FILLED)
+        def _():
+            gather_recv(v3.at[h], v3, c3_s, c3_r, k).wait_recv()
 
     for k in range(1, NH):
         wait_c3(k)
+
+    @pl.when(h < FILLED)
+    def _():
+        for k in range(1, NH):
+            gather_send(v3.at[h], v3, c3_s, c3_r, k).wait_send()
+
     flat3 = jnp.concatenate([v3[c].astype(F32) for c in range(14)], axis=0)
     last3 = jnp.concatenate([flat3[288:432, :64], flat3[288:432, 64:]], axis=0)
     for ab in range(9):

time: 45.9 us -> 45.9 us (level)
  no operation moved by 1% of the time
where the time goes in v9:
time: 45.9 us; the launch traced here: 45.7 us
  Pallas kernels  45.1 us (98%)
  between operations  0.64 us (1%)
    pallas_call x1, Pallas kernels, shards(): pl.pallas_call(kernel, out_shape=(pltpu.VMEM((32, 4, 8, 128), BF16), pltp...  44.2 us

profile of v9, /device:TPU:1, one launch (start us, length us, event | category | flops | bytes accessed | tf_op | source)
XLA Modules:
  0.0 45.7 jit_solution(17584528467512128777)
XLA Ops:
  0.6 44.2 %shard_map.67 = (bf16[32,4,8,128]{3,2,1,0:T(8,128)(2,1)S(1)}, f32[27,32,64]{2,1,0:T(8,128)S(1)}, f32[27,8,64]{2,1,0:T(8,128)S(1)}) custom-call(bf16[32,4,8,128]{3,2,1,0:T(8,128)(2,1)} %x_hbm.1, bf16[27,32,64]{2,1,0:T(8,128)(2,1)} %bitcast.3, bf16[27,8,64]{2,1,0:T(8,128)(2,1)} %f4_hbm.1, bf16[2,4,64,128]{3,2,1,0:T(8,128)(2,1)} %bitcast.4), custom_call_target="tpu_custom_call" | custom-call | tf_op jit(solution)/shard_map/pallas_call | solution.py:698
  44.8 0.9 %shard_map.68 = (bf16[32,4,8,128]{3,2,1,0:T(8,128)(2,1)}, f32[27,32,64]{2,1,0:T(8,128)}, f32[27,8,64]{2,1,0:T(8,128)}) custom-call(bf16[32,4,8,128]{3,2,1,0:T(8,128)(2,1)S(1)} %get-tuple-element.9.gv, f32[27,32,64]{2,1,0:T(8,128)S(1)} %get-tuple-element.10.g3, f32[27,8,64]{2,1,0:T(8,128)S(1)} %get-tuple-element.11.g4), custom_call_target="tpu_custom_call" | custom-call | tf_op jit(solution)/shard_map/pallas_call | solution.py:771

commit v10 on v8

--- a/solution.py
+++ b/solution.py
@@ -277,7 +277,7 @@
     halo_start(*halo_c)
     fetches[2].wait()
     stage("rows_f3", rows_f3)
-    stage("stack_x", lambda: each(0, 4, stack_x))
+    stage("stack_x", lambda: [stack_x(i) for i in range(4)])
     d3[0] = jnp.zeros((10, 64, 128), BF16)
     d3[5] = jnp.zeros((10, 64, 128), BF16)
     d3[:, 0] = jnp.zeros((6, 64, 128), BF16)
@@ -475,12 +475,12 @@
     stage("weight4", weight4)
 
     def pack4(s):
-        rows = pl.ds(pl.multiple_of(8 * s, 8), 8)
-        r4[lax.rem(s, 2), s // 2] = jnp.concatenate(
+        rows = slice(8 * s, 8 * s + 8)
+        r4[s % 2, s // 2] = jnp.concatenate(
             [f4acc[rows, :896], f4acc[rows, 896:]], axis=0
         ).astype(BF16)
 
-    stage("pack4", lambda: each(0, NH, pack4))
+    stage("pack4", lambda: [pack4(s) for s in range(NH)])
     core = lax.rem(h, 2)
     pair = h // 2
 

time: 45.9 us -> 45.7 us (level)
  no operation moved by 1% of the time
where the time goes in v10:
time: 45.7 us; the launch traced here: 45.6 us
  Pallas kernels  44.9 us (98%)
  between operations  0.64 us (1%)
    pallas_call x1, Pallas kernels, shards(): pl.pallas_call(kernel, out_shape=(pltpu.VMEM((32, 4, 8, 128), BF16), pltp...  44 us

profile of v10, /device:TPU:1, one launch (start us, length us, event | category | flops | bytes accessed | tf_op | source)
XLA Modules:
  0.0 45.6 jit_solution(9472483883861256184)
XLA Ops:
  0.6 44.0 %shard_map.67 = (bf16[32,4,8,128]{3,2,1,0:T(8,128)(2,1)S(1)}, f32[27,32,64]{2,1,0:T(8,128)S(1)}, f32[27,8,64]{2,1,0:T(8,128)S(1)}) custom-call(bf16[32,4,8,128]{3,2,1,0:T(8,128)(2,1)} %x_hbm.1, bf16[27,32,64]{2,1,0:T(8,128)(2,1)} %bitcast.3, bf16[27,8,64]{2,1,0:T(8,128)(2,1)} %f4_hbm.1, bf16[2,4,64,128]{3,2,1,0:T(8,128)(2,1)} %bitcast.4), custom_call_target="tpu_custom_call" | custom-call | tf_op jit(solution)/shard_map/pallas_call | solution.py:673
  44.7 0.9 %shard_map.68 = (bf16[32,4,8,128]{3,2,1,0:T(8,128)(2,1)}, f32[27,32,64]{2,1,0:T(8,128)}, f32[27,8,64]{2,1,0:T(8,128)}) custom-call(bf16[32,4,8,128]{3,2,1,0:T(8,128)(2,1)S(1)} %get-tuple-element.9.gv, f32[27,32,64]{2,1,0:T(8,128)S(1)} %get-tuple-element.10.g3, f32[27,8,64]{2,1,0:T(8,128)S(1)} %get-tuple-element.11.g4), custom_call_target="tpu_custom_call" | custom-call | tf_op jit(solution)/shard_map/pallas_call | solution.py:746
